TPU v7x, 512 devices: a whole 4x4x16 slice. The times are simulated.
512 devices in a mesh: row: 64 (over x, y, z_hi), col: 8 (over z_lo, core).
Axes of the slice: x: 4, y: 4, z: 16 (z_hi: 4, z_lo: 4; z = z_hi * 4 + z_lo), core: 2. Of those that a mesh axis runs over, the one named last changes fastest.
Arguments:
- tokens: bfloat16 [320, 12288], P('row'), may hold values from -6 to 6
- weight: bfloat16 [12288, 24576], P('row', 'col'), may hold values from -0.0546875 to 0.0546875
- bias: float32 [24576], P('col'), may hold values from -5 to 5
- grad_out: bfloat16 [320, 24576], P('row', 'col'), may hold values from -6 to 6
Outputs:
- activation: bfloat16 [320, 24576], P('row', 'col')
- input_grad: bfloat16 [320, 12288], P('row')
- weight_grad: bfloat16 [12288, 24576], P('row', 'col')
- bias_grad: float32 [24576], P('col')
All inputs are finite; a program needn't handle non-finite values.
Results may differ from a plain program's by a relative error of at most 0.019.
Values may be sent and summed in bfloat16 or wider, within the bound.
No kernel may reach another device: no remote copies, remote signals or barrier semaphores. Data moves between devices by JAX's collectives and lax.ppermute only.
A program may use at most 64 MiB of HBM per device.

v0:
```python
import math

import jax
import jax.numpy as jnp
from jax import lax
from jax.sharding import PartitionSpec as P

root_coeff = math.sqrt(2.0 / math.pi)
cubic_coeff = 0.044715


def gelu_parts(pre_act):
    argument = root_coeff * (pre_act + cubic_coeff * pre_act * pre_act * pre_act)
    tangent = jnp.tanh(argument)
    output_value = 0.5 * pre_act * (1.0 + tangent)
    derivative = 0.5 * (1.0 + tangent) + 0.5 * pre_act * (1.0 - tangent * tangent) * root_coeff * (
        1.0 + 3.0 * cubic_coeff * pre_act * pre_act
    )
    return (output_value, derivative)


def per_device(tokens, weight, bias, grad_out):
    block_rows = tokens.shape[0]
    token_panel = lax.all_to_all(tokens, "row", split_axis=1, concat_axis=0, tiled=True)
    all_rows = token_panel.shape[0]
    row_block = token_panel
    pre_act = (
        lax.psum_scatter(
            jnp.dot(row_block, weight, preferred_element_type=jnp.float32),
            "row",
            scatter_dimension=0,
            tiled=True,
        )
        + bias
    )
    output_value, derivative = gelu_parts(pre_act)
    activation = output_value.astype(jnp.bfloat16)
    grad_pre = (grad_out.astype(jnp.float32) * derivative).astype(jnp.bfloat16)
    bias_grad = lax.psum(jnp.sum(grad_pre.astype(jnp.float32), axis=0), "row")
    shard_rows = lax.all_gather(grad_pre, "row", axis=0, tiled=True)
    row_block = token_panel
    weight_total = lax.dot_general(
        row_block, shard_rows, (((0,), (0,)), ((), ())), preferred_element_type=jnp.float32
    )
    input_rows = lax.dot_general(
        shard_rows, weight, (((1,), (1,)), ((), ())), preferred_element_type=jnp.float32
    )
    weight_total, input_partial = (weight_total, input_rows)
    panel_width = weight.shape[0]
    input_summed = lax.psum(input_partial.astype(jnp.bfloat16), "col")
    moved = lax.all_to_all(
        input_summed.reshape(all_rows, 1, panel_width),
        "row",
        split_axis=0,
        concat_axis=1,
        tiled=True,
    )
    input_grad = moved.reshape(block_rows, -1)
    return (activation, input_grad, weight_total.astype(jnp.bfloat16), bias_grad)


def solution(mesh):
    placed = (P("row", None), P("row", "col"), P("col"), P("row", "col"))
    return jax.shard_map(
        per_device,
        mesh=mesh,
        in_specs=placed,
        out_specs=(P("row", "col"), P("row", None), P("row", "col"), P("col")),
        check_vma=False,
    )
```

profile of v0, /device:TPU:32, one launch (start us, length us, event | category | flops | bytes accessed | tf_op | source)
XLA Modules:
  0.0 1578.7 jit_solution(1059693074219240977)
XLA Ops:
  7.2 1.3 all_to_all.25
  8.5 0.1 copy.19
  8.6 0.3 reshape.25
  8.9 40.4 %all_to_all.34 = bf16[64,2,480]{2,1,0:T(2,128)(2,1)S(1)} all-to-all(bf16[64,2,480]{2,1,0:T(2,128)(2,1)S(1)} %reshape.25), channel_id=1, replica_groups=mesh['row'=64,'col'=8] {'row'}, dimensions={0} | all-to-all | bytes 245760 | tf_op jit(solution)/shard_map/all_to_all | solution.py:24
  49.2 0.2 reshape.26
  49.5 0.1 all_to_all.28
  49.7 2.6 fusion.10
  52.3 1.3 dynamic-slice
  54.2 855.2 %all-reduce.6.cloned.1.call-done = f32[320,3072]{1,0:T(8,128)} async-done(((f32[320,3072]{1,0:T(8,128)}), f32[320,3072]{1,0:T(8,128)}) %all-reduce.6.cloned.1.call-update) | async-done | bytes 3932176
  909.4 1.7 convert_reduce_fusion
  911.2 119.1 %all-gather.3.cloned.1.call-done = bf16[64,5,3072]{2,1,0:T(8,128)(2,1)} async-done(((bf16[1,5,3072]{2,1,0:T(8,128)(2,1)}), bf16[64,5,3072]{2,1,0:T(8,128)(2,1)}) %all-gather.3.cloned.1.call-update) | async-done | bytes 1966096 | tf_op jit(solution)/shard_map/all_gather | solution.py:40
  1030.3 3.0 reshape.22
  1033.3 1.6 fusion.1
  1035.0 73.4 %all-reduce.4.cloned.1.call-done = bf16[320,1,192]{0,2,1:T(8,128)(2,1)} async-done(((bf16[320,1,192]{0,2,1:T(8,128)(2,1)}), bf16[320,1,192]{0,2,1:T(8,128)(2,1)}) %all-reduce.4.cloned.1.call-update) | async-done | bytes 122896 | tf_op jit(solution)/shard_map/psum | solution.py:50
  1108.4 0.5 broadcast.23
  1108.9 2.3 reduce.1
  1111.2 1.0 copy.20
  1112.2 0.9 reshape.27
  1113.1 17.1 %all-to-all-start.1 = ((bf16[64,2,480]{2,1,0:T(2,128)(2,1)}), bf16[64,2,480]{2,1,0:T(2,128)(2,1)S(1)}, u32[]{:S(2)}, u32[]{:S(2)}) async-start(bf16[64,2,480]{2,1,0:T(2,128)(2,1)} %reshape.27), calls=%async_computation.1 | async-start | bytes 262144 | tf_op jit(solution)/shard_map/all_to_all | solution.py:51
  1130.1 437.8 %psum.15 = f32[3072]{0:T(1024)} all-reduce(f32[3072]{0:T(1024)S(1)} %get-tuple-element.4), channel_id=1, replica_groups=mesh['row'=64,'col'=8] {'row'}, use_global_device_ids=true, to_apply=%region_3.0 | all-reduce | flops 3072 | bytes 24576 | tf_op jit(solution)/shard_map/psum | solution.py:39
  1568.0 1.8 fusion
  1569.8 0.3 reshape.28
  1570.1 1.0 reduce
  1571.2 0.9 reshape.20
  (16 shorter events, 0.3 us)
Async XLA Ops:
  7.2 42.5 %copy-start = (bf16[192,3072]{1,0:T(8,128)(2,1)S(1)}, bf16[192,3072]{1,0:T(8,128)(2,1)}, u32[]{:S(2)}) copy-start(bf16[192,3072]{1,0:T(8,128)(2,1)} %param.5) | copy-start | bytes 3538948
  7.2 902.2 %all-reduce.6.cloned.1.call-start = ((), (), s32[]{:S(2)}) async-start(), calls=%async_computation.4 | async-start | bytes 7864320
  52.2 857.2 %copy-start.1 = (bf16[5,3072]{1,0:T(8,128)(2,1)S(1)}, bf16[5,3072]{1,0:T(8,128)(2,1)}, u32[]{:S(2)}) copy-start(bf16[5,3072]{1,0:T(8,128)(2,1)} %param.7) | copy-start | bytes 92164
  52.2 857.2 %copy-start.2 = (f32[3072]{0:T(1024)S(1)}, f32[3072]{0:T(1024)}, u32[]{:S(2)}) copy-start(f32[3072]{0:T(1024)} %param.6) | copy-start | bytes 36868
  52.3 978.0 %all-gather.3.cloned.1.call-start = ((), (), s32[]{:S(2)}) async-start(), calls=%async_computation.3 | async-start | bytes 3194880 | tf_op jit(solution)/shard_map/all_gather | solution.py:40
  911.1 197.2 %all-reduce.4.cloned.1.call-start = ((), (), s32[]{:S(2)}) async-start(), calls=%async_computation.2 | async-start | bytes 294912 | tf_op jit(solution)/shard_map/psum | solution.py:50
  1113.1 456.7 %all-to-all-start.1 = ((bf16[64,2,480]{2,1,0:T(2,128)(2,1)}), bf16[64,2,480]{2,1,0:T(2,128)(2,1)S(1)}, u32[]{:S(2)}, u32[]{:S(2)}) async-start(bf16[64,2,480]{2,1,0:T(2,128)(2,1)} %reshape.27), calls=%async_computation.1 | async-start | bytes 262144 | tf_op jit(solution)/shard_map/all_to_all | solution.py:51
Sparse Core Ops, SparseCore 0:
  52.4 856.9 all-reduce.5
  914.9 115.3 all-gather.2
  1035.1 73.2 all-reduce.3
where the time goes:
time: 1580 us
  waiting for transfers between devices  1050 us (66%)
  blocking collectives  478 us (30%)
  starting transfers between devices  17.2 us (1%)
    unnamed x4, waiting for transfers between devices  855 us
    psum x1, blocking collectives, per_device(): bias_grad = lax.psum(jnp.sum(grad_pre.astype(jnp.float32), axis=0), 'row')  438 us
    all_gather x1, waiting for transfers between devices, per_device(): shard_rows = lax.all_gather(grad_pre, 'row', axis=0, tiled=True)  119 us
    psum x1, waiting for transfers between devices, per_device(): input_summed = lax.psum(input_partial.astype(jnp.bfloat16), 'col')  73.4 us
    all_to_all x1, blocking collectives, per_device(): lax.all_to_all(tokens, 'row', split_axis=1, concat_axis=0, tiled=True)  40.4 us
  transfers between devices with their start and end apart: 4, of which 3 were waited for; matrix products, arithmetic and copies ran while one was open for 0% of the time, Pallas kernels for 0%

commit v1 on v0

v1 whole, which is shorter than its diff:
```python
import math

import jax
import jax.numpy as jnp
from jax import lax
from jax.sharding import PartitionSpec as P

root_coeff = math.sqrt(2.0 / math.pi)
cubic_coeff = 0.044715

N_XY, N_Z, N_COL = 16, 4, 8
XY_GROUPS = [[p * N_Z + z for p in range(N_XY)] for z in range(N_Z)]
Z_GROUPS = [[p * N_Z + z for z in range(N_Z)] for p in range(N_XY)]
LANES = 128


def gelu_parts(pre_act):
    argument = root_coeff * (pre_act + cubic_coeff * pre_act * pre_act * pre_act)
    tangent = jnp.tanh(argument)
    output_value = 0.5 * pre_act * (1.0 + tangent)
    derivative = 0.5 * (1.0 + tangent) + 0.5 * pre_act * (1.0 - tangent * tangent) * root_coeff * (
        1.0 + 3.0 * cubic_coeff * pre_act * pre_act
    )
    return (output_value, derivative)


def swap_xy(block):
    return lax.all_to_all(block, "row", 0, 0, axis_index_groups=XY_GROUPS)


def swap_z(block):
    return lax.all_to_all(block, "row", 0, 0, axis_index_groups=Z_GROUPS)


def per_device(tokens, weight, bias, grad_out):
    rows, features = tokens.shape
    panel, hidden = weight.shape
    all_rows = rows * N_XY * N_Z
    f32, bf16 = jnp.float32, jnp.bfloat16

    with jax.named_scope("tokens_xy"):
        t = tokens.reshape(rows, N_XY, N_Z * panel).transpose(1, 0, 2)
        t = swap_xy(t.reshape(N_XY, -1, LANES))
    with jax.named_scope("tokens_z"):
        t = t.reshape(N_XY * rows, N_Z, panel).transpose(1, 0, 2)
        t = swap_z(t.reshape(N_Z, -1, LANES))
        t = t.reshape(N_Z, N_XY, rows, panel).transpose(1, 0, 2, 3)
        token_panel = t.reshape(all_rows, panel)
    with jax.named_scope("pre_dot"):
        partial = jnp.dot(token_panel, weight, preferred_element_type=f32).astype(bf16)
        partial = partial.reshape(N_XY, -1, LANES)
    with jax.named_scope("pre_xy"):
        partial = swap_xy(partial)
        partial = jnp.sum(partial.astype(f32), axis=0).astype(bf16)
    with jax.named_scope("pre_z"):
        partial = swap_z(partial.reshape(N_Z, -1, LANES))
        pre_act = jnp.sum(partial.astype(f32), axis=0)
    with jax.named_scope("gelu"):
        pre_act = (pre_act.reshape(rows, -1, LANES) + bias.reshape(-1, LANES)).reshape(-1, LANES)
        output_value, derivative = gelu_parts(pre_act)
        activation = output_value.astype(bf16).reshape(rows, hidden)
        grad_pre = (grad_out.reshape(-1, LANES).astype(f32) * derivative).astype(bf16)
    with jax.named_scope("grad_z"):
        g = swap_z(jnp.broadcast_to(grad_pre[None], (N_Z,) + grad_pre.shape))
    with jax.named_scope("grad_xy"):
        g = g.reshape(-1, LANES)
        g = swap_xy(jnp.broadcast_to(g[None], (N_XY,) + g.shape))
        g = g.reshape(all_rows, hidden)
    with jax.named_scope("input_dot"):
        part = lax.dot_general(g, weight, (((1,), (1,)), ((), ())), preferred_element_type=f32).astype(bf16)
    with jax.named_scope("input_col"):
        slim = panel // N_COL
        part = part.reshape(all_rows, N_COL, slim).transpose(1, 0, 2).reshape(N_COL, -1, LANES)
        part = lax.all_to_all(part, "col", 0, 0)
        part = jnp.sum(part.astype(f32), axis=0).astype(bf16)
    with jax.named_scope("input_row"):
        part = lax.all_to_all(part.reshape(N_XY * N_Z, rows * slim), "row", 0, 0)
    with jax.named_scope("input_back"):
        part = part.reshape(-1, LANES)
        part = lax.all_to_all(jnp.broadcast_to(part[None], (N_COL,) + part.shape), "col", 0, 0)
        part = part.reshape(N_COL, N_XY * N_Z, rows, slim).transpose(2, 1, 0, 3)
        input_grad = part.reshape(rows, features)
    with jax.named_scope("weight_dot"):
        weight_grad = lax.dot_general(token_panel, g, (((0,), (0,)), ((), ())), preferred_element_type=f32).astype(bf16)
    with jax.named_scope("bias_sum"):
        bias_grad = jnp.sum(g.astype(f32), axis=0)
    return (activation, input_grad, weight_grad, bias_grad)


def solution(mesh):
    placed = (P("row", None), P("row", "col"), P("col"), P("row", "col"))
    return jax.shard_map(
        per_device,
        mesh=mesh,
        in_specs=placed,
        out_specs=(P("row", "col"), P("row", None), P("row", "col"), P("col")),
        check_vma=False,
    )
```

time: 1580 us -> 192 us (0.12)
  the two profiles are of different devices: /device:TPU:32 before, /device:TPU:1 now
where the time goes in v1:
time: 192 us; the launch traced here: 191 us
  blocking collectives  105 us (55%)
  waiting for transfers between devices  34.3 us (18%)
  starting transfers between devices  28.6 us (15%)
  local copies, waits for them, and re-layouts  15.6 us (8%)
  other arithmetic  3.61 us (2%)
  matrix products  3.44 us (2%)
    all_to_all x3, blocking collectives, swap_xy(): return lax.all_to_all(block, 'row', 0, 0, axis_index_groups=XY_GROUPS)  63.6 us
    all_to_all x2, blocking collectives, swap_z(): return lax.all_to_all(block, 'row', 0, 0, axis_index_groups=Z_GROUPS)  41.2 us
    all_to_all x1, waiting for transfers between devices, per_device(): part = lax.all_to_all(part.reshape(N_XY * N_Z, rows * slim), 'row', 0, 0)  14 us
    all_to_all x1, waiting for transfers between devices, swap_z(): return lax.all_to_all(block, 'row', 0, 0, axis_index_groups=Z_GROUPS)  12 us
    all_to_all x1, starting transfers between devices, per_device(): part = lax.all_to_all(part, 'col', 0, 0)  11.5 us
    all_to_all x1, starting transfers between devices, per_device(): part = lax.all_to_all(part.reshape(N_XY * N_Z, rows * slim), 'row', 0, 0)  6.47 us
    all_to_all x1, starting transfers between devices, per_device(): lax.all_to_all(jnp.broadcast_to(part[None], (N_COL,) + part.shape), 'col'...  5.67 us
    all_to_all x1, waiting for transfers between devices, per_device(): part = lax.all_to_all(part, 'col', 0, 0)  5.19 us
  transfers between devices with their start and end apart: 4, of which 4 were waited for; matrix products, arithmetic and copies ran while one was open for 3% of the time, Pallas kernels for 0%

profile of v1, /device:TPU:1, one launch (start us, length us, event | category | flops | bytes accessed | tf_op | source)
XLA Modules:
  0.0 191.0 jit_solution(6814222863983550387)
XLA Ops:
  0.6 1.2 reshape.102
  1.8 14.1 %all_to_all.50 = bf16[16,30,128]{2,1,0:T(8,128)(2,1)S(1)} all-to-all(bf16[16,30,128]{2,1,0:T(8,128)(2,1)S(1)} %reshape.102), channel_id=1, replica_groups={{0,32,64,96,128,160,192,224,256,288,320,352,384,416,448,480},{8,40,72,1..., dimensions={0} | all-to-all | bytes 245760 | tf_op jit(solution)/shard_map/tokens_xy/all_to_all | solution.py:28
  16.3 26.8 %all_to_all.51 = bf16[4,120,128]{2,1,0:T(8,128)(2,1)S(1)} all-to-all(bf16[4,120,128]{2,1,0:T(8,128)(2,1)S(1)} %reshape.104), channel_id=1, replica_groups={{0,8,16,24},{32,40,48,56},{64,72,80,88},{96,104,112,120},{128,136,144,1..., dimensions={0} | all-to-all | bytes 245760 | tf_op jit(solution)/shard_map/tokens_z/all_to_all | solution.py:32
  44.2 1.9 %reshape.107 = bf16[16,480,128]{2,1,0:T(8,128)(2,1)} reshape(bf16[320,3072]{1,0:T(8,128)(2,1)S(1)} %convolution_convert_fusion) | data formatting | bytes 3932160 | tf_op jit(solution)/shard_map/pre_dot/reshape | solution.py:51
  46.1 25.9 %all_to_all.52 = bf16[16,480,128]{2,1,0:T(8,128)(2,1)S(1)} all-to-all(bf16[16,480,128]{2,1,0:T(8,128)(2,1)} %reshape.107), channel_id=1, replica_groups={{0,32,64,96,128,160,192,224,256,288,320,352,384,416,448,480},{8,40,72,1..., dimensions={0} | all-to-all | bytes 3932160 | tf_op jit(solution)/shard_map/pre_xy/all_to_all | solution.py:28
  72.0 0.9 reduce_sum.44
  72.9 5.0 %all-to-all-start.3 = ((bf16[4,120,128]{2,1,0:T(8,128)(2,1)}), bf16[4,120,128]{2,1,0:T(8,128)(2,1)S(1)}, u32[]{:S(2)}, u32[]{:S(2)}) async-start(bf16[4,120,128]{2,1,0:T(8,128)(2,1)} %bitcast.4), calls=%async_computation.3 | async-start | bytes 245760 | tf_op jit(solution)/shard_map/pre_z/all_to_all | solution.py:32
  77.9 12.0 %all-to-all-done.3 = bf16[4,120,128]{2,1,0:T(8,128)(2,1)S(1)} async-done(((bf16[4,120,128]{2,1,0:T(8,128)(2,1)}), bf16[4,120,128]{2,1,0:T(8,128)(2,1)S(1)}, u32[]{:S(2)}, u32[]{:S(2)}) %all-to-all-start.3) | async-done | bytes 122912 | tf_op jit(solution)/shard_map/pre_z/all_to_all | solution.py:32
  90.1 14.4 %all_to_all.53 = bf16[4,120,128]{2,1,0:T(8,128)(2,1)S(1)} all-to-all(bf16[4,120,128]{2,1,0:T(8,128)(2,1)S(1)} %broadcast_in_dim.20), channel_id=1, replica_groups={{0,8,16,24},{32,40,48,56},{64,72,80,88},{96,104,112,120},{128,136,144,1..., dimensions={0} | all-to-all | bytes 245760 | tf_op jit(solution)/shard_map/grad_z/all_to_all | solution.py:32
  104.7 23.6 %all_to_all.54 = bf16[16,480,128]{2,1,0:T(8,128)(2,1)} all-to-all(bf16[16,480,128]{2,1,0:T(8,128)(2,1)S(1)} %broadcast_in_dim.22), channel_id=1, replica_groups={{0,32,64,96,128,160,192,224,256,288,320,352,384,416,448,480},{8,40,72,1..., dimensions={0} | all-to-all | bytes 3932160 | tf_op jit(solution)/shard_map/grad_xy/all_to_all | solution.py:28
  128.3 2.8 %reshape.109 = bf16[320,3072]{1,0:T(8,128)(2,1)S(1)} reshape(bf16[16,480,128]{2,1,0:T(8,128)(2,1)} %all_to_all.54) | data formatting | bytes 3932160 | tf_op jit(solution)/shard_map/grad_xy/reshape | solution.py:68
  131.0 0.9 convolution_convert_fusion.2
  132.0 1.1 copy.27
  133.1 2.6 %reshape.111 = bf16[8,60,128]{2,1,0:T(8,128)(2,1)} reshape(bf16[8,320,24]{2,1,0:T(8,128)(2,1)} %bitcast.26) | data formatting | bytes 245760 | tf_op jit(solution)/shard_map/input_col/reshape | solution.py:73
  135.7 11.5 %all-to-all-start.6 = ((bf16[8,60,128]{2,1,0:T(8,128)(2,1)}), bf16[8,60,128]{2,1,0:T(8,128)(2,1)S(1)}, u32[]{:S(2)}, u32[]{:S(2)}) async-start(bf16[8,60,128]{2,1,0:T(8,128)(2,1)} %reshape.111), calls=%async_computation.6 | async-start | bytes 262144 | tf_op jit(solution)/shard_map/input_col/all_to_all | solution.py:74
  147.8 5.2 %all-to-all-done.6 = bf16[8,60,128]{2,1,0:T(8,128)(2,1)S(1)} async-done(((bf16[8,60,128]{2,1,0:T(8,128)(2,1)}), bf16[8,60,128]{2,1,0:T(8,128)(2,1)S(1)}, u32[]{:S(2)}, u32[]{:S(2)}) %all-to-all-start.6) | async-done | bytes 122912 | tf_op jit(solution)/shard_map/input_col/all_to_all | solution.py:74
  153.8 6.5 %all-to-all-start.7 = ((bf16[64,1,120]{2,1,0:T(2,128)(2,1)}), bf16[64,1,120]{2,1,0:T(2,128)(2,1)S(1)}, u32[]{:S(2)}, u32[]{:S(2)}) async-start(bf16[64,1,120]{2,1,0:T(2,128)(2,1)} %all_to_all.40), calls=%async_computation.7 | async-start | bytes 65536 | tf_op jit(solution)/shard_map/input_row/all_to_all | solution.py:77
  160.3 1.6 fusion.5
  161.8 14.0 %all-to-all-done.7 = bf16[64,1,120]{2,1,0:T(2,128)(2,1)S(1)} async-done(((bf16[64,1,120]{2,1,0:T(2,128)(2,1)}), bf16[64,1,120]{2,1,0:T(2,128)(2,1)S(1)}, u32[]{:S(2)}, u32[]{:S(2)}) %all-to-all-start.7) | async-done | bytes 15392 | tf_op jit(solution)/shard_map/input_row/all_to_all | solution.py:77
  176.7 5.7 %all-to-all-start.8 = ((bf16[8,60,128]{2,1,0:T(8,128)(2,1)}), bf16[8,60,128]{2,1,0:T(8,128)(2,1)S(1)}, u32[]{:S(2)}, u32[]{:S(2)}) async-start(bf16[8,60,128]{2,1,0:T(8,128)(2,1)} %broadcast_in_dim.24), calls=%async_computation.8 | async-start | bytes 262144 | tf_op jit(solution)/shard_map/input_back/all_to_all | solution.py:80
  182.4 0.9 convert_reduce_fusion
  183.3 1.8 fusion
  185.1 3.1 %all-to-all-done.8 = bf16[8,60,128]{2,1,0:T(8,128)(2,1)S(1)} async-done(((bf16[8,60,128]{2,1,0:T(8,128)(2,1)}), bf16[8,60,128]{2,1,0:T(8,128)(2,1)S(1)}, u32[]{:S(2)}, u32[]{:S(2)}) %all-to-all-start.8) | async-done | bytes 122912 | tf_op jit(solution)/shard_map/input_back/all_to_all | solution.py:80
  189.5 1.5 reshape.113
  (26 shorter events, 5.4 us)
Async XLA Ops:
  0.6 42.9 %copy-start = (bf16[192,3072]{1,0:T(8,128)(2,1)S(1)}, bf16[192,3072]{1,0:T(8,128)(2,1)}, u32[]{:S(2)}) copy-start(bf16[192,3072]{1,0:T(8,128)(2,1)} %param.5) | copy-start | bytes 3538948
  72.0 5.9 %copy-start.1 = (bf16[5,3072]{1,0:T(8,128)(2,1)S(1)}, bf16[5,3072]{1,0:T(8,128)(2,1)}, u32[]{:S(2)}) copy-start(bf16[5,3072]{1,0:T(8,128)(2,1)} %param.7) | copy-start | bytes 92164
  72.0 18.0 %copy-start.2 = (f32[3072]{0:T(1024)S(1)}, f32[3072]{0:T(1024)}, u32[]{:S(2)}) copy-start(f32[3072]{0:T(1024)} %param.6) | copy-start | bytes 36868
  72.9 17.1 %all-to-all-start.3 = ((bf16[4,120,128]{2,1,0:T(8,128)(2,1)}), bf16[4,120,128]{2,1,0:T(8,128)(2,1)S(1)}, u32[]{:S(2)}, u32[]{:S(2)}) async-start(bf16[4,120,128]{2,1,0:T(8,128)(2,1)} %bitcast.4), calls=%async_computation.3 | async-start | bytes 245760 | tf_op jit(solution)/shard_map/pre_z/all_to_all | solution.py:32
  135.7 17.3 %all-to-all-start.6 = ((bf16[8,60,128]{2,1,0:T(8,128)(2,1)}), bf16[8,60,128]{2,1,0:T(8,128)(2,1)S(1)}, u32[]{:S(2)}, u32[]{:S(2)}) async-start(bf16[8,60,128]{2,1,0:T(8,128)(2,1)} %reshape.111), calls=%async_computation.6 | async-start | bytes 262144 | tf_op jit(solution)/shard_map/input_col/all_to_all | solution.py:74
  153.8 22.0 %all-to-all-start.7 = ((bf16[64,1,120]{2,1,0:T(2,128)(2,1)}), bf16[64,1,120]{2,1,0:T(2,128)(2,1)S(1)}, u32[]{:S(2)}, u32[]{:S(2)}) async-start(bf16[64,1,120]{2,1,0:T(2,128)(2,1)} %all_to_all.40), calls=%async_computation.7 | async-start | bytes 65536 | tf_op jit(solution)/shard_map/input_row/all_to_all | solution.py:77
  176.7 11.5 %all-to-all-start.8 = ((bf16[8,60,128]{2,1,0:T(8,128)(2,1)}), bf16[8,60,128]{2,1,0:T(8,128)(2,1)S(1)}, u32[]{:S(2)}, u32[]{:S(2)}) async-start(bf16[8,60,128]{2,1,0:T(8,128)(2,1)} %broadcast_in_dim.24), calls=%async_computation.8 | async-start | bytes 262144 | tf_op jit(solution)/shard_map/input_back/all_to_all | solution.py:80

commit v2 on v1

v2 whole, which is shorter than its diff:
```python
import math

import jax
import jax.numpy as jnp
from jax import lax
from jax.experimental import pallas as pl
from jax.experimental.pallas import tpu as pltpu
from jax.sharding import PartitionSpec as P

root_coeff = math.sqrt(2.0 / math.pi)
cubic_coeff = 0.044715

N_XY, N_Z, N_COL, N_ROW = 16, 4, 8, 64
LANES = 128
XY_GROUPS = [[p * N_Z + z for p in range(N_XY)] for z in range(N_Z)]
Z_GROUPS = [[p * N_Z + z for z in range(N_Z)] for p in range(N_XY)]
BOTH = ("row", "col")


def turned(row, chunk):
    low, core = divmod(chunk, 2)
    return row * N_COL + ((low + row) % 4) * 2 + core


ROW_GROUPS = [[turned(r, j) for r in range(N_ROW)] for j in range(N_COL)]
COL_GROUPS = [[turned(r, j) for j in range(N_COL)] for r in range(N_ROW)]


def gelu_parts(pre_act):
    argument = root_coeff * (pre_act + cubic_coeff * pre_act * pre_act * pre_act)
    tangent = jnp.tanh(argument)
    output_value = 0.5 * pre_act * (1.0 + tangent)
    derivative = 0.5 * (1.0 + tangent) + 0.5 * pre_act * (1.0 - tangent * tangent) * root_coeff * (
        1.0 + 3.0 * cubic_coeff * pre_act * pre_act
    )
    return (output_value, derivative)


def swap(block, axis, groups):
    return lax.all_to_all(block, axis, 0, 0, axis_index_groups=groups)


def in_vmem(value):
    return pltpu.with_memory_space_constraint(value, pltpu.VMEM)


WHOLE = pl.BlockSpec(memory_space=pltpu.VMEM)
PARAMS = pltpu.CompilerParams(vmem_limit_bytes=24 * 2**20)


def pre_kernel(t_ref, w_ref, o_ref, s_ref):
    rows, hidden = t_ref.shape[0], w_ref.shape[1]
    lines = hidden // LANES
    for j in range(0, lines, 2):
        both = jnp.dot(t_ref[...], w_ref[:, j * LANES : (j + 2) * LANES], preferred_element_type=jnp.float32)
        s_ref[pl.ds(j, rows, stride=lines), :] = both[:, :LANES]
        s_ref[pl.ds(j + 1, rows, stride=lines), :] = both[:, LANES:]
    o_ref[...] = s_ref[...].astype(o_ref.dtype).reshape(o_ref.shape)


def pre_dot(token_panel, weight):
    rows, hidden = token_panel.shape[0], weight.shape[1]
    lines = rows * hidden // LANES
    return pl.pallas_call(
        pre_kernel,
        out_shape=pltpu.VMEM((N_XY, lines // N_XY, LANES), jnp.bfloat16),
        in_specs=[WHOLE, WHOLE],
        out_specs=WHOLE,
        scratch_shapes=[pltpu.VMEM((lines, LANES), jnp.float32)],
        compiler_params=PARAMS,
        cost_estimate=pl.CostEstimate(flops=2 * rows * hidden * weight.shape[0], bytes_accessed=4 * 2**20, transcendentals=0),
        name="pre_dot",
    )(in_vmem(token_panel), weight)


def sum_kernel(x_ref, o_ref):
    step = 96
    for b in range(0, o_ref.shape[0], step):
        total = x_ref[0, b : b + step, :].astype(jnp.float32)
        for p in range(1, x_ref.shape[0]):
            total += x_ref[p, b : b + step, :].astype(jnp.float32)
        o_ref[b : b + step, :] = total.astype(o_ref.dtype)


def sum_parts(parts):
    return pl.pallas_call(
        sum_kernel,
        out_shape=pltpu.VMEM(parts.shape[1:], jnp.bfloat16),
        in_specs=[WHOLE],
        out_specs=WHOLE,
        compiler_params=PARAMS,
        cost_estimate=pl.CostEstimate(flops=parts.size, bytes_accessed=2 * parts.size, transcendentals=0),
        name="sum_parts",
    )(in_vmem(parts))


def post_kernel(g_ref, w_ref, rows_ref, part_ref, s_ref):
    rows, hidden = rows_ref.shape
    lines = hidden // LANES
    s_ref[...] = g_ref[...].reshape(s_ref.shape).astype(jnp.float32)
    for j in range(lines):
        rows_ref[:, j * LANES : (j + 1) * LANES] = s_ref[pl.ds(j, rows, stride=lines), :].astype(rows_ref.dtype)
    part_ref[...] = lax.dot_general(
        w_ref[...], rows_ref[...], (((1,), (1,)), ((), ())), preferred_element_type=jnp.float32
    ).astype(part_ref.dtype)


def post_dot(gathered, weight):
    panel, hidden = weight.shape
    rows = gathered.size // hidden
    return pl.pallas_call(
        post_kernel,
        out_shape=(pltpu.VMEM((rows, hidden), jnp.bfloat16), pltpu.VMEM((panel, rows), jnp.bfloat16)),
        in_specs=[WHOLE, WHOLE],
        out_specs=(WHOLE, WHOLE),
        scratch_shapes=[pltpu.VMEM((gathered.size // LANES, LANES), jnp.float32)],
        compiler_params=PARAMS,
        cost_estimate=pl.CostEstimate(flops=2 * rows * hidden * panel, bytes_accessed=6 * 2**20, transcendentals=0),
        name="post_dot",
    )(in_vmem(gathered), weight)


def per_device(tokens, weight, bias, grad_out):
    rows, features = tokens.shape
    panel, hidden = weight.shape
    all_rows = rows * N_ROW
    f32, bf16 = jnp.float32, jnp.bfloat16

    with jax.named_scope("tokens"):
        t = tokens.reshape(rows, N_ROW, panel).transpose(1, 0, 2)
        t = swap(t.reshape(N_ROW, 8, -1), BOTH, ROW_GROUPS)
        token_panel = t.reshape(all_rows, panel)
    with jax.named_scope("pre_dot"):
        partial = pre_dot(token_panel, weight)
    with jax.named_scope("pre_xy"):
        partial = swap(partial, "row", XY_GROUPS)
        partial = sum_parts(partial)
    with jax.named_scope("pre_z"):
        partial = swap(partial.reshape(N_Z, -1, LANES), "row", Z_GROUPS)
        pre_act = jnp.sum(partial.astype(f32), axis=0)
    with jax.named_scope("gelu"):
        pre_act = (pre_act.reshape(rows, -1, LANES) + bias.reshape(-1, LANES)).reshape(-1, LANES)
        output_value, derivative = gelu_parts(pre_act)
        activation = output_value.astype(bf16).reshape(rows, hidden)
        grad_pre = (grad_out.reshape(-1, LANES).astype(f32) * derivative).astype(bf16)
    with jax.named_scope("grad_z"):
        g = swap(jnp.broadcast_to(grad_pre[None], (N_Z,) + grad_pre.shape), "row", Z_GROUPS)
    with jax.named_scope("grad_xy"):
        g = g.reshape(-1, LANES)
        g = swap(jnp.broadcast_to(g[None], (N_XY,) + g.shape), "row", XY_GROUPS)
    with jax.named_scope("input_dot"):
        g, part = post_dot(g, weight)
    with jax.named_scope("input_col"):
        part = swap(part.reshape(N_COL, -1, all_rows), BOTH, COL_GROUPS)
        part = jnp.sum(part.astype(f32), axis=0).astype(bf16)
    with jax.named_scope("input_row"):
        slim = panel // N_COL
        part = part.reshape(slim, N_ROW, rows).transpose(1, 2, 0).reshape(N_ROW, rows * slim)
        part = swap(part, BOTH, ROW_GROUPS)
    with jax.named_scope("input_back"):
        part = part.reshape(N_ROW, rows, slim).transpose(1, 0, 2).reshape(-1, LANES)
        part = swap(jnp.broadcast_to(part[None], (N_COL,) + part.shape), BOTH, COL_GROUPS)
        part = part.reshape(N_COL, rows, N_ROW, slim).transpose(1, 2, 0, 3)
        input_grad = part.reshape(rows, features)
    with jax.named_scope("weight_dot"):
        weight_grad = lax.dot_general(token_panel, g, (((0,), (0,)), ((), ())), preferred_element_type=f32).astype(bf16)
    with jax.named_scope("bias_sum"):
        bias_grad = jnp.sum(g.astype(f32), axis=0)
    return (activation, input_grad, weight_grad, bias_grad)


def solution(mesh):
    placed = (P("row", None), P("row", "col"), P("col"), P("row", "col"))
    return jax.shard_map(
        per_device,
        mesh=mesh,
        in_specs=placed,
        out_specs=(P("row", "col"), P("row", None), P("row", "col"), P("col")),
        check_vma=False,
    )
```

time: 192 us -> 182 us (0.948)
  local copies, waits for them, and re-layouts: 15.6 us -> 7.11 us
  Pallas kernels: 0 us -> 4.02 us
  blocking collectives: 105 us -> 102 us
  other arithmetic: 3.61 us -> 1.69 us
    reshape x9 -> x5, local copies, waits for them, and re-layouts: 10.9 us -> 2.54 us  [the longest x2 1.36 us: per_device(): t = tokens.reshape(rows, N_ROW, panel).transpose(1, 0, 2)]
    pallas_call x0 -> x3, Pallas kernels: none -> 4.02 us  [the longest x1 2.12 us: post_dot(): pl.pallas_call(post_kernel, out_shape=(pltpu.VMEM((rows, hidden), jnp.bfl...]
    all_to_all x5 -> x4, blocking collectives: 105 us -> 102 us  [swap(): return lax.all_to_all(block, axis, 0, 0, axis_index_groups=groups)]
  transfers between devices with their start and end apart: 4 -> 4, of which waited for: 4 -> 4; matrix products, arithmetic and copies ran while one was open for 3% -> 2% of each run, Pallas kernels for 0% -> 0%
where the time goes in v2:
time: 182 us; the launch traced here: 181 us
  blocking collectives  102 us (56%)
  waiting for transfers between devices  34.8 us (19%)
  starting transfers between devices  29.2 us (16%)
  local copies, waits for them, and re-layouts  7.11 us (4%)
  Pallas kernels  4.02 us (2%)
  matrix products  1.83 us (1%)
    all_to_all x4, blocking collectives, swap(): return lax.all_to_all(block, axis, 0, 0, axis_index_groups=groups)  102 us
    all_to_all x4, waiting for transfers between devices, swap(): return lax.all_to_all(block, axis, 0, 0, axis_index_groups=groups)  34.8 us
    all_to_all x4, starting transfers between devices, swap(): return lax.all_to_all(block, axis, 0, 0, axis_index_groups=groups)  29.2 us
  transfers between devices with their start and end apart: 4, of which 4 were waited for; matrix products, arithmetic and copies ran while one was open for 2% of the time, Pallas kernels for 0%

profile of v2, /device:TPU:1, one launch (start us, length us, event | category | flops | bytes accessed | tf_op | source)
XLA Modules:
  0.0 181.0 jit_solution(15527859575223049914)
XLA Ops:
  0.6 1.3 reshape.89
  2.3 36.4 %all_to_all.44 = bf16[64,8,120]{2,1,0:T(8,128)(2,1)S(1)} all-to-all(bf16[64,8,120]{2,1,0:T(8,128)(2,1)S(1)} %reshape.90), channel_id=1, replica_groups={{0,10,20,30,32,42,52,62,64,74,84,94,96,106,116,126,128,138,148,158,160,..., dimensions={0} | all-to-all | bytes 245760 | tf_op jit(solution)/shard_map/tokens/all_to_all | solution.py:40
  38.9 1.0 pre_dot.1
  39.9 26.3 %all_to_all.45.x_ref = bf16[16,480,128]{2,1,0:T(8,128)(2,1)S(1)} all-to-all(bf16[16,480,128]{2,1,0:T(8,128)(2,1)S(1)} %pre_dot.1), channel_id=1, replica_groups={{0,32,64,96,128,160,192,224,256,288,320,352,384,416,448,480},{8,40,72,1..., dimensions={0} | all-to-all | bytes 3932160 | tf_op jit(solution)/shard_map/pre_xy/all_to_all | solution.py:40
  66.2 0.9 sum_parts.1
  67.1 6.3 %all-to-all-start.2 = ((bf16[4,120,128]{2,1,0:T(8,128)(2,1)}), bf16[4,120,128]{2,1,0:T(8,128)(2,1)S(1)}, u32[]{:S(2)}, u32[]{:S(2)}) async-start(bf16[4,120,128]{2,1,0:T(8,128)(2,1)} %bitcast.1), calls=%async_computation.2 | async-start | bytes 245760 | tf_op jit(solution)/shard_map/pre_z/all_to_all | solution.py:40
  73.4 12.7 %all-to-all-done.2 = bf16[4,120,128]{2,1,0:T(8,128)(2,1)S(1)} async-done(((bf16[4,120,128]{2,1,0:T(8,128)(2,1)}), bf16[4,120,128]{2,1,0:T(8,128)(2,1)S(1)}, u32[]{:S(2)}, u32[]{:S(2)}) %all-to-all-start.2) | async-done | bytes 122912 | tf_op jit(solution)/shard_map/pre_z/all_to_all | solution.py:40
  86.3 15.5 %all_to_all.46 = bf16[4,120,128]{2,1,0:T(8,128)(2,1)S(1)} all-to-all(bf16[4,120,128]{2,1,0:T(8,128)(2,1)S(1)} %broadcast_in_dim.20), channel_id=1, replica_groups={{0,8,16,24},{32,40,48,56},{64,72,80,88},{96,104,112,120},{128,136,144,1..., dimensions={0} | all-to-all | bytes 245760 | tf_op jit(solution)/shard_map/grad_z/all_to_all | solution.py:40
  102.1 23.4 %all_to_all.47.g_ref = bf16[16,480,128]{2,1,0:T(8,128)(2,1)S(1)} all-to-all(bf16[16,480,128]{2,1,0:T(8,128)(2,1)S(1)} %broadcast_in_dim.22), channel_id=1, replica_groups={{0,32,64,96,128,160,192,224,256,288,320,352,384,416,448,480},{8,40,72,1..., dimensions={0} | all-to-all | bytes 3932160 | tf_op jit(solution)/shard_map/grad_xy/all_to_all | solution.py:40
  125.5 2.1 %post_dot.1 = (bf16[320,3072]{1,0:T(8,128)(2,1)S(1)}, bf16[192,320]{1,0:T(8,128)(2,1)}) custom-call(bf16[16,480,128]{2,1,0:T(8,128)(2,1)S(1)} %all_to_all.47.g_ref, bf16[192,3072]{1,0:T(8,128)(2,1)S(1)} %copy-done), custom_call_target="tpu_custom_call" | custom-call | flops 377487360 | bytes 6291456 | tf_op jit(solution)/shard_map/input_dot/post_dot/pallas_call | solution.py:111
  127.6 11.4 %all-to-all-start.5 = ((bf16[8,24,320]{2,1,0:T(8,128)(2,1)}), bf16[8,24,320]{2,1,0:T(8,128)(2,1)S(1)}, u32[]{:S(2)}, u32[]{:S(2)}) async-start(bf16[8,24,320]{2,1,0:T(8,128)(2,1)} %bitcast.5), calls=%async_computation.5 | async-start | bytes 294912 | tf_op jit(solution)/shard_map/input_col/all_to_all | solution.py:40
  139.0 5.9 %all-to-all-done.5 = bf16[8,24,320]{2,1,0:T(8,128)(2,1)S(1)} async-done(((bf16[8,24,320]{2,1,0:T(8,128)(2,1)}), bf16[8,24,320]{2,1,0:T(8,128)(2,1)S(1)}, u32[]{:S(2)}, u32[]{:S(2)}) %all-to-all-start.5) | async-done | bytes 122912 | tf_op jit(solution)/shard_map/input_col/all_to_all | solution.py:40
  145.2 0.7 copy.16
  146.0 5.9 %all-to-all-start.6 = ((bf16[64,1,120]{2,1,0:T(2,128)(2,1)}), bf16[64,1,120]{2,1,0:T(2,128)(2,1)S(1)}, u32[]{:S(2)}, u32[]{:S(2)}) async-start(bf16[64,1,120]{2,1,0:T(2,128)(2,1)} %copy.16), calls=%async_computation.6 | async-start | bytes 65536 | tf_op jit(solution)/shard_map/input_row/all_to_all | solution.py:40
  151.9 0.7 fusion.5
  152.5 13.1 %all-to-all-done.6 = bf16[64,1,120]{2,1,0:T(2,128)(2,1)S(1)} async-done(((bf16[64,1,120]{2,1,0:T(2,128)(2,1)}), bf16[64,1,120]{2,1,0:T(2,128)(2,1)S(1)}, u32[]{:S(2)}, u32[]{:S(2)}) %all-to-all-start.6) | async-done | bytes 15392 | tf_op jit(solution)/shard_map/input_row/all_to_all | solution.py:40
  166.0 0.7 broadcast_in_dim.24
  166.7 5.6 %all-to-all-start.7 = ((bf16[8,60,128]{2,1,0:T(8,128)(2,1)}), bf16[8,60,128]{2,1,0:T(8,128)(2,1)S(1)}, u32[]{:S(2)}, u32[]{:S(2)}) async-start(bf16[8,60,128]{2,1,0:T(8,128)(2,1)} %broadcast_in_dim.24), calls=%async_computation.7 | async-start | bytes 262144 | tf_op jit(solution)/shard_map/input_back/all_to_all | solution.py:40
  172.3 0.9 convert_reduce_fusion
  173.2 1.8 %fusion = bf16[192,3072]{1,0:T(8,128)(2,1)} fusion(bf16[320,3072]{1,0:T(8,128)(2,1)S(1)} %get-tuple-element.7, bf16[320,192]{1,0:T(8,128)(2,1)S(1)} %reshape.91.t_ref), kind=kOutput, calls=%fused_computation.2 | convolution fusion | flops 378077184 | bytes 3268608 | tf_op jit(solution)/shard_map/weight_dot/dot_general | solution.py:166
  175.0 3.1 %all-to-all-done.7 = bf16[8,60,128]{2,1,0:T(8,128)(2,1)S(1)} async-done(((bf16[8,60,128]{2,1,0:T(8,128)(2,1)}), bf16[8,60,128]{2,1,0:T(8,128)(2,1)S(1)}, u32[]{:S(2)}, u32[]{:S(2)}) %all-to-all-start.7) | async-done | bytes 122912 | tf_op jit(solution)/shard_map/input_back/all_to_all | solution.py:40
  178.1 0.9 reshape.96
  179.0 0.4 copy.19
  179.4 1.5 reshape.97
  (22 shorter events, 1.7 us)
Async XLA Ops:
  0.6 38.3 %copy-start = (bf16[192,3072]{1,0:T(8,128)(2,1)S(1)}, bf16[192,3072]{1,0:T(8,128)(2,1)}, u32[]{:S(2)}) copy-start(bf16[192,3072]{1,0:T(8,128)(2,1)} %w_ref.3) | copy-start | bytes 3538948
  66.2 7.2 %copy-start.1 = (bf16[5,3072]{1,0:T(8,128)(2,1)S(1)}, bf16[5,3072]{1,0:T(8,128)(2,1)}, u32[]{:S(2)}) copy-start(bf16[5,3072]{1,0:T(8,128)(2,1)} %param.7) | copy-start | bytes 92164
  66.2 20.0 %copy-start.2 = (f32[3072]{0:T(1024)S(1)}, f32[3072]{0:T(1024)}, u32[]{:S(2)}) copy-start(f32[3072]{0:T(1024)} %param.6) | copy-start | bytes 36868
  67.1 19.1 %all-to-all-start.2 = ((bf16[4,120,128]{2,1,0:T(8,128)(2,1)}), bf16[4,120,128]{2,1,0:T(8,128)(2,1)S(1)}, u32[]{:S(2)}, u32[]{:S(2)}) async-start(bf16[4,120,128]{2,1,0:T(8,128)(2,1)} %bitcast.1), calls=%async_computation.2 | async-start | bytes 245760 | tf_op jit(solution)/shard_map/pre_z/all_to_all | solution.py:40
  127.6 17.3 %all-to-all-start.5 = ((bf16[8,24,320]{2,1,0:T(8,128)(2,1)}), bf16[8,24,320]{2,1,0:T(8,128)(2,1)S(1)}, u32[]{:S(2)}, u32[]{:S(2)}) async-start(bf16[8,24,320]{2,1,0:T(8,128)(2,1)} %bitcast.5), calls=%async_computation.5 | async-start | bytes 294912 | tf_op jit(solution)/shard_map/input_col/all_to_all | solution.py:40
  146.0 19.7 %all-to-all-start.6 = ((bf16[64,1,120]{2,1,0:T(2,128)(2,1)}), bf16[64,1,120]{2,1,0:T(2,128)(2,1)S(1)}, u32[]{:S(2)}, u32[]{:S(2)}) async-start(bf16[64,1,120]{2,1,0:T(2,128)(2,1)} %copy.16), calls=%async_computation.6 | async-start | bytes 65536 | tf_op jit(solution)/shard_map/input_row/all_to_all | solution.py:40
  166.7 11.4 %all-to-all-start.7 = ((bf16[8,60,128]{2,1,0:T(8,128)(2,1)}), bf16[8,60,128]{2,1,0:T(8,128)(2,1)S(1)}, u32[]{:S(2)}, u32[]{:S(2)}) async-start(bf16[8,60,128]{2,1,0:T(8,128)(2,1)} %broadcast_in_dim.24), calls=%async_computation.7 | async-start | bytes 262144 | tf_op jit(solution)/shard_map/input_back/all_to_all | solution.py:40

commit v3 on v2

v3 whole, which is shorter than its diff:
```python
import functools
import math

import jax
import jax.numpy as jnp
from jax import lax
from jax.experimental import pallas as pl
from jax.experimental.pallas import tpu as pltpu
from jax.sharding import PartitionSpec as P

root_coeff = math.sqrt(2.0 / math.pi)
cubic_coeff = 0.044715

N_PAIR, N_HALF, N_YZ, N_Z, N_COL, N_ROW = 2, 2, 16, 4, 8, 64
N_PY = 8
LANES = 128
TAIL = 16
BOTH = ("row", "col")


def row_of(pair, half, yz):
    return (pair * N_HALF + half) * N_YZ + yz


def turned(row, chunk):
    low, core = divmod(chunk, 2)
    return row * N_COL + ((low + row) % 4) * 2 + core


ROW_GROUPS = [[turned(r, j) for r in range(N_ROW)] for j in range(N_COL)]
COL_GROUPS = [[turned(r, j) for j in range(N_COL)] for r in range(N_ROW)]
PAIR_COL_GROUPS = [
    [turned(row_of(p, i, yz), j) for i in range(N_HALF) for j in range(N_COL)] for p in range(N_PAIR) for yz in range(N_YZ)
]
PY_GROUPS = [
    [row_of(p, i, y * N_Z + z) for p in range(N_PAIR) for y in range(N_YZ // N_Z)] for i in range(N_HALF) for z in range(N_Z)
]
Z_GROUPS = [[q * N_Z + z for z in range(N_Z)] for q in range(N_ROW // N_Z)]
PARTNER = [(r, r ^ N_YZ) for r in range(N_ROW)]


def gelu_parts(pre_act):
    argument = root_coeff * (pre_act + cubic_coeff * pre_act * pre_act * pre_act)
    tangent = jnp.tanh(argument)
    output_value = 0.5 * pre_act * (1.0 + tangent)
    derivative = 0.5 * (1.0 + tangent) + 0.5 * pre_act * (1.0 - tangent * tangent) * root_coeff * (
        1.0 + 3.0 * cubic_coeff * pre_act * pre_act
    )
    return (output_value, derivative)


def swap(block, axis, groups):
    return lax.all_to_all(block, axis, 0, 0, axis_index_groups=groups)


def in_vmem(value):
    return pltpu.with_memory_space_constraint(value, pltpu.VMEM)


WHOLE = pl.BlockSpec(memory_space=pltpu.VMEM)
SCALAR = pl.BlockSpec(memory_space=pltpu.SMEM)
PARAMS = pltpu.CompilerParams(vmem_limit_bytes=24 * 2**20)


def weight_kernel(half_ref, w_ref, got_ref, o_ref):
    panel, width = o_ref.shape[1:]
    o_ref[0] = w_ref[:, pl.ds(pl.multiple_of(half_ref[0] * width, LANES), width)]
    o_ref[1] = got_ref[:panel, :]


def both_panels(half, weight, got):
    panel, width = weight.shape[0], got.shape[1]
    return pl.pallas_call(
        weight_kernel,
        out_shape=pltpu.VMEM((N_HALF, panel, width), jnp.bfloat16),
        in_specs=[SCALAR, WHOLE, WHOLE],
        out_specs=WHOLE,
        compiler_params=PARAMS,
        cost_estimate=pl.CostEstimate(flops=0, bytes_accessed=3 * 2**20, transcendentals=0),
        name="both_panels",
    )(half, weight, got)


def pre_kernel(own_ref, other_ref, w_ref, o_ref, s_ref):
    rows = own_ref.shape[0]
    lines = w_ref.shape[2] // LANES
    for j in range(0, lines, 2):
        columns = slice(j * LANES, (j + 2) * LANES)
        both = jnp.dot(own_ref[...], w_ref[0, :, columns], preferred_element_type=jnp.float32)
        both += jnp.dot(other_ref[...], w_ref[1, :, columns], preferred_element_type=jnp.float32)
        s_ref[pl.ds(j, rows, stride=lines), :] = both[:, :LANES]
        s_ref[pl.ds(j + 1, rows, stride=lines), :] = both[:, LANES:]
    o_ref[...] = s_ref[...].astype(o_ref.dtype).reshape(o_ref.shape)


def pre_dot(own, other, weights):
    rows, (_, panel, width) = own.shape[0], weights.shape
    lines = rows * width // LANES
    return pl.pallas_call(
        pre_kernel,
        out_shape=pltpu.VMEM((N_PY, lines // N_PY, LANES), jnp.bfloat16),
        in_specs=[WHOLE, WHOLE, WHOLE],
        out_specs=WHOLE,
        scratch_shapes=[pltpu.VMEM((lines, LANES), jnp.float32)],
        compiler_params=PARAMS,
        cost_estimate=pl.CostEstimate(flops=4 * rows * width * panel, bytes_accessed=4 * 2**20, transcendentals=0),
        name="pre_dot",
    )(in_vmem(own), in_vmem(other), in_vmem(weights))


def sum_kernel(x_ref, o_ref):
    step = 96
    for b in range(0, o_ref.shape[0], step):
        total = x_ref[0, b : b + step, :].astype(jnp.float32)
        for p in range(1, x_ref.shape[0]):
            total += x_ref[p, b : b + step, :].astype(jnp.float32)
        o_ref[b : b + step, :] = total.astype(o_ref.dtype)


def sum_parts(parts):
    return pl.pallas_call(
        sum_kernel,
        out_shape=pltpu.VMEM(parts.shape[1:], jnp.bfloat16),
        in_specs=[WHOLE],
        out_specs=WHOLE,
        compiler_params=PARAMS,
        cost_estimate=pl.CostEstimate(flops=parts.size, bytes_accessed=2 * parts.size, transcendentals=0),
        name="sum_parts",
    )(in_vmem(parts))


def post_kernel(half_ref, g_ref, w_ref, rows_ref, part_ref, s_ref):
    rows, width = rows_ref.shape
    lines = width // LANES
    s_ref[...] = g_ref[...].reshape(s_ref.shape).astype(jnp.float32)
    for j in range(lines):
        rows_ref[:, j * LANES : (j + 1) * LANES] = s_ref[pl.ds(j, rows, stride=lines), :].astype(rows_ref.dtype)
    for k, place in enumerate((half_ref[0], 1 - half_ref[0])):
        part_ref[place] = lax.dot_general(
            w_ref[k], rows_ref[...], (((1,), (1,)), ((), ())), preferred_element_type=jnp.float32
        ).astype(part_ref.dtype)


def post_dot(half, gathered, weights):
    _, panel, width = weights.shape
    rows = gathered.size // width
    return pl.pallas_call(
        post_kernel,
        out_shape=(pltpu.VMEM((rows, width), jnp.bfloat16), jax.ShapeDtypeStruct((N_HALF, panel, rows), jnp.bfloat16)),
        in_specs=[SCALAR, WHOLE, WHOLE],
        out_specs=(WHOLE, WHOLE),
        scratch_shapes=[pltpu.VMEM((gathered.size // LANES, LANES), jnp.float32)],
        compiler_params=PARAMS,
        cost_estimate=pl.CostEstimate(flops=4 * rows * width * panel, bytes_accessed=6 * 2**20, transcendentals=0),
        name="post_dot",
    )(half, in_vmem(gathered), in_vmem(weights))


def join_kernel(half_ref, w_ref, act_ref, bias_ref, back_ref, w_out, act_out, bias_out):
    panel, width = w_ref.shape
    rows = act_ref.shape[0]
    mine = pl.ds(pl.multiple_of(half_ref[0] * width, LANES), width)
    theirs = pl.ds(pl.multiple_of((1 - half_ref[0]) * width, LANES), width)
    w_out[:, mine] = w_ref[...]
    w_out[:, theirs] = back_ref[:panel, :]
    tail = back_ref[panel:, :].astype(jnp.float32)
    act_out[:, mine] = act_ref[...]
    act_out[:, theirs] = tail[:rows].astype(act_out.dtype)
    bias_out[:, mine] = bias_ref[...]
    bias_out[:, theirs] = tail[rows : rows + 1] + tail[rows + 1 : rows + 2] + tail[rows + 2 : rows + 3]


def join_halves(half, weight_own, act_own, bias_own, back):
    panel, width = weight_own.shape
    hidden, rows = N_HALF * width, act_own.shape[0]
    return pl.pallas_call(
        join_kernel,
        out_shape=(
            jax.ShapeDtypeStruct((panel, hidden), jnp.bfloat16),
            jax.ShapeDtypeStruct((rows, hidden), jnp.bfloat16),
            jax.ShapeDtypeStruct((1, hidden), jnp.float32),
        ),
        in_specs=[SCALAR, WHOLE, WHOLE, WHOLE, WHOLE],
        out_specs=(WHOLE, WHOLE, WHOLE),
        compiler_params=PARAMS,
        cost_estimate=pl.CostEstimate(flops=2**20, bytes_accessed=3 * 2**20, transcendentals=0),
        name="join_halves",
    )(half, weight_own, act_own, bias_own, back)


def interleave_kernel(slim, x_ref, o_ref, s_ref):
    groups, lines = x_ref.shape[0], x_ref.shape[1]
    rows = o_ref.shape[0]
    step = lines // rows
    s_ref[...] = x_ref[...].astype(jnp.float32)
    values = [
        jnp.concatenate([s_ref[c, pl.ds(m, rows, stride=step), :] for m in range(step)], 1) for c in range(groups)
    ]
    for r in range(0, N_ROW, 2):
        pieces = [values[c][:, q * slim : (q + 1) * slim] for q in (r, r + 1) for c in range(groups)]
        width = len(pieces) * slim
        o_ref[:, r // 2 * width : (r // 2 + 1) * width] = jnp.concatenate(pieces, 1).astype(o_ref.dtype)


def interleave(parts, rows, slim):
    groups, lines, _ = parts.shape
    return pl.pallas_call(
        functools.partial(interleave_kernel, slim),
        out_shape=jax.ShapeDtypeStruct((rows, groups * lines // rows * LANES), jnp.bfloat16),
        in_specs=[WHOLE],
        out_specs=WHOLE,
        scratch_shapes=[pltpu.VMEM((groups, lines, LANES), jnp.float32)],
        compiler_params=PARAMS,
        cost_estimate=pl.CostEstimate(flops=2**20, bytes_accessed=2**19, transcendentals=0),
        name="interleave",
    )(parts)


def per_device(tokens, weight, bias, grad_out):
    rows, features = tokens.shape
    panel, hidden = weight.shape
    all_rows = rows * N_ROW
    width = hidden // N_HALF
    f32, bf16 = jnp.float32, jnp.bfloat16
    half = (lax.axis_index("row") // N_YZ) % N_HALF
    first = half == 0
    half_ref = half.reshape(1).astype(jnp.int32)

    def columns(value, which):
        return lax.dynamic_slice_in_dim(value, which * width, width, value.ndim - 1)

    def in_order(own, other, axis):
        return jnp.concatenate([jnp.where(first, own, other), jnp.where(first, other, own)], axis)

    with jax.named_scope("weight_in"):
        give = jnp.concatenate([columns(weight, 1 - half), columns(grad_out, 1 - half)], 0)
        got = lax.ppermute(give, "row", PARTNER)
        weights = both_panels(half_ref, weight, got)
    with jax.named_scope("tokens"):
        t = tokens.reshape(rows, N_ROW, panel).transpose(1, 0, 2).reshape(N_ROW, 8, -1)
        flipped = t.reshape(N_PAIR, N_HALF, N_YZ, 8, -1)[:, ::-1].reshape(t.shape)
        t = swap(jnp.concatenate([t, flipped], 1), BOTH, ROW_GROUPS)

        def token_rows(value):
            value = value.reshape(N_PAIR, N_HALF, N_YZ, rows, panel).transpose(0, 2, 1, 3, 4)
            return value.reshape(all_rows, panel)

        own, other = token_rows(t[:, :8]), token_rows(t[:, 8:])
    with jax.named_scope("pre_dot"):
        partial = pre_dot(own, other, weights)
    with jax.named_scope("pre_xy"):
        partial = swap(partial, "row", PY_GROUPS)
        partial = sum_parts(partial)
    with jax.named_scope("pre_z"):
        partial = swap(partial.reshape(N_Z, -1, LANES), "row", Z_GROUPS)
        pre_act = jnp.sum(partial.astype(f32), axis=0)
    with jax.named_scope("gelu"):
        pair_rows = N_HALF * rows
        bias_half = columns(bias, half).reshape(-1, LANES)
        pre_act = (pre_act.reshape(pair_rows, -1, LANES) + bias_half).reshape(-1, LANES)
        output_value, derivative = gelu_parts(pre_act)
        activation = output_value.astype(bf16)
        upstream = in_order(columns(grad_out, half), got[panel:], 0).reshape(-1, LANES)
        grad_pre = (upstream.astype(f32) * derivative).astype(bf16)
        activation, grad_pre = lax.optimization_barrier((activation, grad_pre))
    with jax.named_scope("grad_z"):
        g = swap(jnp.broadcast_to(grad_pre[None], (N_Z,) + grad_pre.shape), "row", Z_GROUPS)
    with jax.named_scope("grad_xy"):
        g = g.reshape(-1, LANES)
        g = swap(jnp.broadcast_to(g[None], (N_PY,) + g.shape), "row", PY_GROUPS)
        g, activation = lax.optimization_barrier((g, activation))
        activation = activation.reshape(N_HALF, rows, width)
    with jax.named_scope("input_dot"):
        g, part = post_dot(half_ref, g, weights)
    with jax.named_scope("weight_dot"):
        over_rows = (((0,), (0,)), ((), ()))
        weight_own = lax.dot_general(own, g, over_rows, preferred_element_type=f32).astype(bf16)
        weight_other = lax.dot_general(other, g, over_rows, preferred_element_type=f32).astype(bf16)
    with jax.named_scope("bias_sum"):
        bias_half = jnp.sum(g.astype(f32), axis=0)
        high = lax.reduce_precision(bias_half, 8, 7)
        middle = lax.reduce_precision(bias_half - high, 8, 7)
        low = bias_half - high - middle
        pieces = jnp.stack([high, middle, low] + [jnp.zeros_like(low)] * (TAIL - rows - 3)).astype(bf16)
    with jax.named_scope("input_col"):
        slim = panel // N_COL
        part = swap(part.reshape(N_HALF * N_COL, slim, all_rows), BOTH, PAIR_COL_GROUPS)
        part = jnp.sum(part.astype(f32), axis=0).astype(bf16)
    with jax.named_scope("weight_out"):
        give = jnp.concatenate([weight_other, lax.dynamic_index_in_dim(activation, 1 - half, 0, False), pieces], 0)
        part, give = lax.optimization_barrier((part, give))
        back = lax.ppermute(give, "row", PARTNER)
    with jax.named_scope("input_row"):
        part = part.reshape(slim, N_PAIR, N_YZ, N_HALF, rows).transpose(1, 3, 2, 4, 0).reshape(N_ROW, rows * slim)
        part = swap(part, BOTH, ROW_GROUPS)
    with jax.named_scope("input_back"):
        part = part.reshape(N_ROW, rows, slim).transpose(1, 0, 2).reshape(-1, LANES)
        part = swap(jnp.broadcast_to(part[None], (N_COL,) + part.shape), BOTH, COL_GROUPS)
        act_own = lax.dynamic_index_in_dim(activation, half, 0, False)
        outs = join_halves(half_ref, weight_own, act_own, bias_half.reshape(1, -1), back)
        part, weight_grad, activation, bias_grad = lax.optimization_barrier((part,) + tuple(outs))
        bias_grad = bias_grad.reshape(hidden)
        input_grad = interleave(part, rows, slim)
    return (activation, input_grad, weight_grad, bias_grad)


def solution(mesh):
    placed = (P("row", None), P("row", "col"), P("col"), P("row", "col"))
    return jax.shard_map(
        per_device,
        mesh=mesh,
        in_specs=placed,
        out_specs=(P("row", "col"), P("row", None), P("row", "col"), P("col")),
        check_vma=False,
    )
```

time: 182 us -> 179 us (0.984)
  blocking collectives: 102 us -> 52.4 us
  starting transfers between devices: 29.2 us -> 55.8 us
  waiting for transfers between devices: 34.8 us -> 56.1 us
  Pallas kernels: 4.02 us -> 6.46 us
  local copies, waits for them, and re-layouts: 7.11 us -> 4.83 us
    all_to_all x4 -> x3, blocking collectives: 102 us -> 52.4 us  [swap(): return lax.all_to_all(block, axis, 0, 0, axis_index_groups=groups)]
    all_to_all x4 -> x5, starting transfers between devices: 29.2 us -> 50.3 us  [swap(): return lax.all_to_all(block, axis, 0, 0, axis_index_groups=groups)]
    ppermute x0 -> x2, waiting for transfers between devices: none -> 15.7 us  [the longest x1 15.7 us: per_device(): got = lax.ppermute(give, 'row', PARTNER)]
    all_to_all x4 -> x5, waiting for transfers between devices: 34.8 us -> 40.4 us  [swap(): return lax.all_to_all(block, axis, 0, 0, axis_index_groups=groups)]
    ppermute x0 -> x2, starting transfers between devices: none -> 5.54 us  [the longest x1 2.93 us: per_device(): got = lax.ppermute(give, 'row', PARTNER)]
    pallas_call x2 -> x5, Pallas kernels: 3.11 us -> 5.69 us  [the longest x1 1.78 us: post_dot(): pl.pallas_call(post_kernel, out_shape=(pltpu.VMEM((rows, width), jnp.bflo...]
    reshape x7 -> x10, local copies, waits for them, and re-layouts: 4.28 us -> 2.73 us  [the longest x3 1.53 us: per_device(): tokens.reshape(rows, N_ROW, panel).transpose(1, 0, 2).reshape(N_ROW, 8, -1)]
  transfers between devices with their start and end apart: 4 -> 7, of which waited for: 4 -> 6; matrix products, arithmetic and copies ran while one was open for 2% -> 2% of each run, Pallas kernels for 0% -> 1%
where the time goes in v3:
time: 179 us
  waiting for transfers between devices  56.1 us (31%)
  starting transfers between devices  55.8 us (31%)
  blocking collectives  52.4 us (29%)
  Pallas kernels  6.46 us (4%)
  local copies, waits for them, and re-layouts  4.83 us (3%)
    all_to_all x3, blocking collectives, swap(): return lax.all_to_all(block, axis, 0, 0, axis_index_groups=groups)  52.4 us
    all_to_all x5, starting transfers between devices, swap(): return lax.all_to_all(block, axis, 0, 0, axis_index_groups=groups)  50.3 us
    all_to_all x5, waiting for transfers between devices, swap(): return lax.all_to_all(block, axis, 0, 0, axis_index_groups=groups)  40.4 us
    ppermute x1, waiting for transfers between devices, per_device(): got = lax.ppermute(give, 'row', PARTNER)  15.7 us
  transfers between devices with their start and end apart: 7, of which 6 were waited for; matrix products, arithmetic and copies ran while one was open for 2% of the time, Pallas kernels for 1%

profile of v3, /device:TPU:1, one launch (start us, length us, event | category | flops | bytes accessed | tf_op | source)
XLA Modules:
  0.0 178.8 jit_solution(4500271423514908495)
XLA Ops:
  0.6 1.2 reshape.97
  2.5 0.8 pad_maximum_fusion.1
  3.3 20.9 %all-to-all-start = ((bf16[64,16,120]{2,1,0:T(8,128)(2,1)}), bf16[64,16,120]{2,1,0:T(8,128)(2,1)S(1)}, u32[]{:S(2)}, u32[]{:S(2)}) async-start(bf16[64,16,120]{2,1,0:T(8,128)(2,1)} %pad_maximum_fusion.1), calls=%async_computation | async-start | bytes 524288 | tf_op jit(solution)/shard_map/tokens/all_to_all | solution.py:53
  24.3 2.9 %collective-permute-start = (bf16[197,1536]{1,0:T(8,128)(2,1)S(1)}, bf16[197,1536]{1,0:T(8,128)(2,1)S(1)}, u32[]{:S(2)}, u32[]{:S(2)}) collective-permute-start(bf16[197,1536]{1,0:T(8,128)(2,1)S(1)} %pad_maximum_fusion), channel_id=1, source_target_pairs={{0,128},{8,136},{16,144},{24,152},{32,160},{40,168},{48,176},{56,1... | collective-permute-start | bytes 1815560 | tf_op jit(solution)/shard_map/weight_in/ppermute | solution.py:237
  27.2 15.7 %collective-permute-done.got_ref = bf16[197,1536]{1,0:T(8,128)(2,1)S(1)} collective-permute-done((bf16[197,1536]{1,0:T(8,128)(2,1)S(1)}, bf16[197,1536]{1,0:T(8,128)(2,1)S(1)}, u32[]{:S(2)}, u32[]{:S(2)}) %collective-permute-start) | collective-permute-done | bytes 605216 | tf_op jit(solution)/shard_map/weight_in/ppermute | solution.py:237
  43.0 2.9 %all-to-all-done = bf16[64,16,120]{2,1,0:T(8,128)(2,1)S(1)} async-done(((bf16[64,16,120]{2,1,0:T(8,128)(2,1)}), bf16[64,16,120]{2,1,0:T(8,128)(2,1)S(1)}, u32[]{:S(2)}, u32[]{:S(2)}) %all-to-all-start) | async-done | bytes 245792 | tf_op jit(solution)/shard_map/tokens/all_to_all | solution.py:53
  46.8 1.7 pre_dot.1
  48.5 3.6 %all-to-all-start.1 = ((bf16[8,480,128]{2,1,0:T(8,128)(2,1)}), bf16[8,480,128]{2,1,0:T(8,128)(2,1)S(1)}, u32[]{:S(2)}, u32[]{:S(2)}) async-start(bf16[8,480,128]{2,1,0:T(8,128)(2,1)} %pre_dot.1), calls=%async_computation.1 | async-start | bytes 1966080 | tf_op jit(solution)/shard_map/pre_xy/all_to_all | solution.py:53
  52.2 12.5 %all-to-all-done.1.x_ref = bf16[8,480,128]{2,1,0:T(8,128)(2,1)S(1)} async-done(((bf16[8,480,128]{2,1,0:T(8,128)(2,1)}), bf16[8,480,128]{2,1,0:T(8,128)(2,1)S(1)}, u32[]{:S(2)}, u32[]{:S(2)}) %all-to-all-start.1) | async-done | bytes 983072 | tf_op jit(solution)/shard_map/pre_xy/all_to_all | solution.py:53
  64.6 0.8 sum_parts.1
  65.4 9.5 %all-to-all-start.2 = ((bf16[4,120,128]{2,1,0:T(8,128)(2,1)}), bf16[4,120,128]{2,1,0:T(8,128)(2,1)S(1)}, u32[]{:S(2)}, u32[]{:S(2)}) async-start(bf16[4,120,128]{2,1,0:T(8,128)(2,1)} %bitcast.5), calls=%async_computation.2 | async-start | bytes 245760 | tf_op jit(solution)/shard_map/pre_z/all_to_all | solution.py:53
  74.9 12.0 %all-to-all-done.2 = bf16[4,120,128]{2,1,0:T(8,128)(2,1)S(1)} async-done(((bf16[4,120,128]{2,1,0:T(8,128)(2,1)}), bf16[4,120,128]{2,1,0:T(8,128)(2,1)S(1)}, u32[]{:S(2)}, u32[]{:S(2)}) %all-to-all-start.2) | async-done | bytes 122912 | tf_op jit(solution)/shard_map/pre_z/all_to_all | solution.py:53
  87.0 14.9 %all_to_all.45 = bf16[4,120,128]{2,1,0:T(8,128)(2,1)S(1)} all-to-all(bf16[4,120,128]{2,1,0:T(8,128)(2,1)S(1)} %broadcast_in_dim.20), channel_id=1, replica_groups={{0,8,16,24},{32,40,48,56},{64,72,80,88},{96,104,112,120},{128,136,144,1..., dimensions={0} | all-to-all | bytes 245760 | tf_op jit(solution)/shard_map/grad_z/all_to_all | solution.py:53
  102.1 18.9 %all_to_all.46.g_ref = bf16[8,480,128]{2,1,0:T(8,128)(2,1)S(1)} all-to-all(bf16[8,480,128]{2,1,0:T(8,128)(2,1)S(1)} %broadcast_in_dim.22), channel_id=1, replica_groups={{0,32,64,96,256,288,320,352},{8,40,72,104,264,296,328,360},{16,48,80,11..., dimensions={0} | all-to-all | bytes 1966080 | tf_op jit(solution)/shard_map/grad_xy/all_to_all | solution.py:53
  121.0 1.8 post_dot.1
  122.8 10.9 %all-to-all-start.5 = ((bf16[16,24,320]{2,1,0:T(8,128)(2,1)}), bf16[16,24,320]{2,1,0:T(8,128)(2,1)S(1)}, u32[]{:S(2)}, u32[]{:S(2)}) async-start(bf16[16,24,320]{2,1,0:T(8,128)(2,1)} %bitcast.8), calls=%async_computation.5 | async-start | bytes 589824 | tf_op jit(solution)/shard_map/input_col/all_to_all | solution.py:53
  134.8 8.9 %all-to-all-done.5 = bf16[16,24,320]{2,1,0:T(8,128)(2,1)S(1)} async-done(((bf16[16,24,320]{2,1,0:T(8,128)(2,1)}), bf16[16,24,320]{2,1,0:T(8,128)(2,1)S(1)}, u32[]{:S(2)}, u32[]{:S(2)}) %all-to-all-start.5) | async-done | bytes 245792 | tf_op jit(solution)/shard_map/input_col/all_to_all | solution.py:53
  143.8 2.6 %collective-permute-start.1 = (bf16[208,1536]{1,0:T(8,128)(2,1)S(1)}, bf16[208,1536]{1,0:T(8,128)(2,1)S(1)}, u32[]{:S(2)}, u32[]{:S(2)}) collective-permute-start(bf16[208,1536]{1,0:T(8,128)(2,1)S(1)} %concatenate.16), channel_id=1, source_target_pairs={{0,128},{8,136},{16,144},{24,152},{32,160},{40,168},{48,176},{56,1... | collective-permute-start | bytes 1916936 | tf_op jit(solution)/shard_map/weight_out/ppermute | solution.py:292
  146.7 18.6 %all_to_all.47 = bf16[64,1,120]{2,1,0:T(2,128)(2,1)S(1)} all-to-all(bf16[64,1,120]{2,1,0:T(2,128)(2,1)S(1)} %all_to_all.36), channel_id=1, replica_groups={{0,10,20,30,32,42,52,62,64,74,84,94,96,106,116,126,128,138,148,158,160,..., dimensions={0} | all-to-all | bytes 30720 | tf_op jit(solution)/shard_map/input_row/all_to_all | solution.py:53
  165.7 0.7 broadcast_in_dim.24
  166.4 5.5 %all-to-all-start.7 = ((bf16[8,60,128]{2,1,0:T(8,128)(2,1)}), bf16[8,60,128]{2,1,0:T(8,128)(2,1)S(1)}, u32[]{:S(2)}, u32[]{:S(2)}) async-start(bf16[8,60,128]{2,1,0:T(8,128)(2,1)} %broadcast_in_dim.24), calls=%async_computation.7 | async-start | bytes 262144 | tf_op jit(solution)/shard_map/input_back/all_to_all | solution.py:53
  172.4 1.1 join_halves.1
  173.6 4.2 %all-to-all-done.7.x_ref = bf16[8,60,128]{2,1,0:T(8,128)(2,1)S(1)} async-done(((bf16[8,60,128]{2,1,0:T(8,128)(2,1)}), bf16[8,60,128]{2,1,0:T(8,128)(2,1)S(1)}, u32[]{:S(2)}, u32[]{:S(2)}) %all-to-all-start.7) | async-done | bytes 122912 | tf_op jit(solution)/shard_map/input_back/all_to_all | solution.py:53
  177.7 1.1 interleave.1
  (49 shorter events, 4.4 us)
Async XLA Ops:
  0.6 51.4 %copy-start = (f32[3072]{0:T(1024)S(1)}, f32[3072]{0:T(1024)}, u32[]{:S(2)}) copy-start(f32[3072]{0:T(1024)} %param.6) | copy-start | bytes 36868
  1.9 22.2 %copy-start.1 = (bf16[192,3072]{1,0:T(8,128)(2,1)S(1)}, bf16[192,3072]{1,0:T(8,128)(2,1)}, u32[]{:S(2)}) copy-start(bf16[192,3072]{1,0:T(8,128)(2,1)} %w_ref.1) | copy-start | bytes 3538948
  2.5 21.7 %copy-start.2 = (bf16[5,3072]{1,0:T(8,128)(2,1)S(1)}, bf16[5,3072]{1,0:T(8,128)(2,1)}, u32[]{:S(2)}) copy-start(bf16[5,3072]{1,0:T(8,128)(2,1)} %param.7) | copy-start | bytes 92164
  3.3 42.6 %all-to-all-start = ((bf16[64,16,120]{2,1,0:T(8,128)(2,1)}), bf16[64,16,120]{2,1,0:T(8,128)(2,1)S(1)}, u32[]{:S(2)}, u32[]{:S(2)}) async-start(bf16[64,16,120]{2,1,0:T(8,128)(2,1)} %pad_maximum_fusion.1), calls=%async_computation | async-start | bytes 524288 | tf_op jit(solution)/shard_map/tokens/all_to_all | solution.py:53
  24.3 18.6 %collective-permute-start = (bf16[197,1536]{1,0:T(8,128)(2,1)S(1)}, bf16[197,1536]{1,0:T(8,128)(2,1)S(1)}, u32[]{:S(2)}, u32[]{:S(2)}) collective-permute-start(bf16[197,1536]{1,0:T(8,128)(2,1)S(1)} %pad_maximum_fusion), channel_id=1, source_target_pairs={{0,128},{8,136},{16,144},{24,152},{32,160},{40,168},{48,176},{56,1... | collective-permute-start | bytes 1815560 | tf_op jit(solution)/shard_map/weight_in/ppermute | solution.py:237
  48.5 16.2 %all-to-all-start.1 = ((bf16[8,480,128]{2,1,0:T(8,128)(2,1)}), bf16[8,480,128]{2,1,0:T(8,128)(2,1)S(1)}, u32[]{:S(2)}, u32[]{:S(2)}) async-start(bf16[8,480,128]{2,1,0:T(8,128)(2,1)} %pre_dot.1), calls=%async_computation.1 | async-start | bytes 1966080 | tf_op jit(solution)/shard_map/pre_xy/all_to_all | solution.py:53
  65.4 21.5 %all-to-all-start.2 = ((bf16[4,120,128]{2,1,0:T(8,128)(2,1)}), bf16[4,120,128]{2,1,0:T(8,128)(2,1)S(1)}, u32[]{:S(2)}, u32[]{:S(2)}) async-start(bf16[4,120,128]{2,1,0:T(8,128)(2,1)} %bitcast.5), calls=%async_computation.2 | async-start | bytes 245760 | tf_op jit(solution)/shard_map/pre_z/all_to_all | solution.py:53
  122.8 20.9 %all-to-all-start.5 = ((bf16[16,24,320]{2,1,0:T(8,128)(2,1)}), bf16[16,24,320]{2,1,0:T(8,128)(2,1)S(1)}, u32[]{:S(2)}, u32[]{:S(2)}) async-start(bf16[16,24,320]{2,1,0:T(8,128)(2,1)} %bitcast.8), calls=%async_computation.5 | async-start | bytes 589824 | tf_op jit(solution)/shard_map/input_col/all_to_all | solution.py:53
  143.8 28.6 %collective-permute-start.1 = (bf16[208,1536]{1,0:T(8,128)(2,1)S(1)}, bf16[208,1536]{1,0:T(8,128)(2,1)S(1)}, u32[]{:S(2)}, u32[]{:S(2)}) collective-permute-start(bf16[208,1536]{1,0:T(8,128)(2,1)S(1)} %concatenate.16), channel_id=1, source_target_pairs={{0,128},{8,136},{16,144},{24,152},{32,160},{40,168},{48,176},{56,1... | collective-permute-start | bytes 1916936 | tf_op jit(solution)/shard_map/weight_out/ppermute | solution.py:292
  166.4 11.4 %all-to-all-start.7 = ((bf16[8,60,128]{2,1,0:T(8,128)(2,1)}), bf16[8,60,128]{2,1,0:T(8,128)(2,1)S(1)}, u32[]{:S(2)}, u32[]{:S(2)}) async-start(bf16[8,60,128]{2,1,0:T(8,128)(2,1)} %broadcast_in_dim.24), calls=%async_computation.7 | async-start | bytes 262144 | tf_op jit(solution)/shard_map/input_back/all_to_all | solution.py:53

commit v4 on v3

--- a/solution.py
+++ b/solution.py
@@ -247,6 +247,11 @@
 
         own, other = token_rows(t[:, :8]), token_rows(t[:, 8:])
     with jax.named_scope("pre_dot"):
+        pair_rows = N_HALF * rows
+        bias_half = columns(bias, half).reshape(1, -1, LANES)
+        bias_rows = jnp.broadcast_to(bias_half, (pair_rows,) + bias_half.shape[1:]).reshape(-1, LANES)
+        upstream = in_order(columns(grad_out, half), got[panel:], 0).reshape(-1, LANES)
+        own, other, bias_rows, upstream = lax.optimization_barrier((own, other, bias_rows, upstream))
         partial = pre_dot(own, other, weights)
     with jax.named_scope("pre_xy"):
         partial = swap(partial, "row", PY_GROUPS)
@@ -255,12 +260,9 @@
         partial = swap(partial.reshape(N_Z, -1, LANES), "row", Z_GROUPS)
         pre_act = jnp.sum(partial.astype(f32), axis=0)
     with jax.named_scope("gelu"):
-        pair_rows = N_HALF * rows
-        bias_half = columns(bias, half).reshape(-1, LANES)
-        pre_act = (pre_act.reshape(pair_rows, -1, LANES) + bias_half).reshape(-1, LANES)
+        pre_act = pre_act + bias_rows
         output_value, derivative = gelu_parts(pre_act)
         activation = output_value.astype(bf16)
-        upstream = in_order(columns(grad_out, half), got[panel:], 0).reshape(-1, LANES)
         grad_pre = (upstream.astype(f32) * derivative).astype(bf16)
         activation, grad_pre = lax.optimization_barrier((activation, grad_pre))
     with jax.named_scope("grad_z"):

time: 179 us -> 173 us (0.966)
  blocking collectives: 52.4 us -> 82 us
  waiting for transfers between devices: 56.1 us -> 34.3 us
  starting transfers between devices: 55.8 us -> 42.6 us
    all_to_all x3 -> x5, blocking collectives: 52.4 us -> 82 us  [swap(): return lax.all_to_all(block, axis, 0, 0, axis_index_groups=groups)]
    ppermute x1, waiting for transfers between devices: 15.7 us -> 0.01 us  [per_device(): got = lax.ppermute(give, 'row', PARTNER)]
    all_to_all x5 -> x3, starting transfers between devices: 50.3 us -> 36 us  [swap(): return lax.all_to_all(block, axis, 0, 0, axis_index_groups=groups)]
    all_to_all x5 -> x3, waiting for transfers between devices: 40.4 us -> 34.3 us  [swap(): return lax.all_to_all(block, axis, 0, 0, axis_index_groups=groups)]
  transfers between devices with their start and end apart: 7 -> 5, of which waited for: 6 -> 3; matrix products, arithmetic and copies ran while one was open for 2% -> 3% of each run, Pallas kernels for 1% -> 1%
where the time goes in v4:
time: 173 us; the launch traced here: 172 us
  blocking collectives  82 us (47%)
  starting transfers between devices  42.6 us (25%)
  waiting for transfers between devices  34.3 us (20%)
  local copies, waits for them, and re-layouts  5 us (3%)
  Pallas kernels  4.87 us (3%)
    all_to_all x5, blocking collectives, swap(): return lax.all_to_all(block, axis, 0, 0, axis_index_groups=groups)  82 us
    all_to_all x3, starting transfers between devices, swap(): return lax.all_to_all(block, axis, 0, 0, axis_index_groups=groups)  36 us
    all_to_all x3, waiting for transfers between devices, swap(): return lax.all_to_all(block, axis, 0, 0, axis_index_groups=groups)  34.3 us
    ppermute x1, starting transfers between devices, per_device(): got = lax.ppermute(give, 'row', PARTNER)  3.95 us
  transfers between devices with their start and end apart: 5, of which 3 were waited for; matrix products, arithmetic and copies ran while one was open for 3% of the time, Pallas kernels for 1%

profile of v4, /device:TPU:1, one launch (start us, length us, event | category | flops | bytes accessed | tf_op | source)
XLA Modules:
  0.0 171.9 jit_solution(17566925552908101543)
XLA Ops:
  0.7 1.1 constant_dynamic-slice_fusion.1
  1.9 3.9 %collective-permute-start = (bf16[197,1536]{1,0:T(8,128)(2,1)S(1)}, bf16[197,1536]{1,0:T(8,128)(2,1)S(1)}, u32[]{:S(2)}, u32[]{:S(2)}) collective-permute-start(bf16[197,1536]{1,0:T(8,128)(2,1)S(1)} %pad_maximum_fusion), channel_id=1, source_target_pairs={{0,128},{8,136},{16,144},{24,152},{32,160},{40,168},{48,176},{56,1... | collective-permute-start | bytes 1815560 | tf_op jit(solution)/shard_map/weight_in/ppermute | solution.py:237
  6.8 0.8 pad_maximum_fusion.1
  7.5 19.7 %all-to-all-start = ((bf16[64,16,120]{2,1,0:T(8,128)(2,1)}), bf16[64,16,120]{2,1,0:T(8,128)(2,1)S(1)}, u32[]{:S(2)}, u32[]{:S(2)}) async-start(bf16[64,16,120]{2,1,0:T(8,128)(2,1)} %pad_maximum_fusion.1), calls=%async_computation | async-start | bytes 524288 | tf_op jit(solution)/shard_map/tokens/all_to_all | solution.py:53
  27.6 21.2 %all-to-all-done = bf16[64,16,120]{2,1,0:T(8,128)(2,1)S(1)} async-done(((bf16[64,16,120]{2,1,0:T(8,128)(2,1)}), bf16[64,16,120]{2,1,0:T(8,128)(2,1)S(1)}, u32[]{:S(2)}, u32[]{:S(2)}) %all-to-all-start) | async-done | bytes 245792 | tf_op jit(solution)/shard_map/tokens/all_to_all | solution.py:53
  48.8 0.3 reshape.101
  49.8 0.7 pre_dot.1
  50.5 16.3 %all_to_all.45.x_ref = bf16[8,480,128]{2,1,0:T(8,128)(2,1)S(1)} all-to-all(bf16[8,480,128]{2,1,0:T(8,128)(2,1)S(1)} %pre_dot.1), channel_id=1, replica_groups={{0,32,64,96,256,288,320,352},{8,40,72,104,264,296,328,360},{16,48,80,11..., dimensions={0} | all-to-all | bytes 1966080 | tf_op jit(solution)/shard_map/pre_xy/all_to_all | solution.py:53
  66.9 17.9 %all_to_all.46 = bf16[4,120,128]{2,1,0:T(8,128)(2,1)S(1)} all-to-all(bf16[4,120,128]{2,1,0:T(8,128)(2,1)S(1)} %bitcast.27), channel_id=1, replica_groups={{0,8,16,24},{32,40,48,56},{64,72,80,88},{96,104,112,120},{128,136,144,1..., dimensions={0} | all-to-all | bytes 245760 | tf_op jit(solution)/shard_map/pre_z/all_to_all | solution.py:53
  84.9 14.8 %all_to_all.47 = bf16[4,120,128]{2,1,0:T(8,128)(2,1)S(1)} all-to-all(bf16[4,120,128]{2,1,0:T(8,128)(2,1)S(1)} %broadcast_in_dim.29), channel_id=1, replica_groups={{0,8,16,24},{32,40,48,56},{64,72,80,88},{96,104,112,120},{128,136,144,1..., dimensions={0} | all-to-all | bytes 245760 | tf_op jit(solution)/shard_map/grad_z/all_to_all | solution.py:53
  99.9 15.3 %all_to_all.48.g_ref = bf16[8,480,128]{2,1,0:T(8,128)(2,1)S(1)} all-to-all(bf16[8,480,128]{2,1,0:T(8,128)(2,1)S(1)} %broadcast_in_dim.31), channel_id=1, replica_groups={{0,32,64,96,256,288,320,352},{8,40,72,104,264,296,328,360},{16,48,80,11..., dimensions={0} | all-to-all | bytes 1966080 | tf_op jit(solution)/shard_map/grad_xy/all_to_all | solution.py:53
  115.2 1.8 %post_dot.1 = (bf16[320,1536]{1,0:T(8,128)(2,1)S(1)}, bf16[2,192,320]{2,1,0:T(8,128)(2,1)}) custom-call(s32[1]{0:T(128)} %bitcast.half_ref, bf16[8,480,128]{2,1,0:T(8,128)(2,1)S(1)} %all_to_all.48.g_ref, bf16[2,192,1536]{2,1,0:T(8,128)(2,1)S(1)} %both_panels.1.w_ref), custom_call_target="tpu_custom_call" | custom-call | flops 377487360 | bytes 6291456 | tf_op jit(solution)/shard_map/input_dot/post_dot/pallas_call | solution.py:147
  117.0 11.0 %all-to-all-start.5 = ((bf16[16,24,320]{2,1,0:T(8,128)(2,1)}), bf16[16,24,320]{2,1,0:T(8,128)(2,1)S(1)}, u32[]{:S(2)}, u32[]{:S(2)}) async-start(bf16[16,24,320]{2,1,0:T(8,128)(2,1)} %bitcast.8), calls=%async_computation.5 | async-start | bytes 589824 | tf_op jit(solution)/shard_map/input_col/all_to_all | solution.py:53
  128.2 0.5 convolution_convert_fusion.1
  128.8 0.3 concatenate.16
  129.1 8.9 %all-to-all-done.5 = bf16[16,24,320]{2,1,0:T(8,128)(2,1)S(1)} async-done(((bf16[16,24,320]{2,1,0:T(8,128)(2,1)}), bf16[16,24,320]{2,1,0:T(8,128)(2,1)S(1)}, u32[]{:S(2)}, u32[]{:S(2)}) %all-to-all-start.5) | async-done | bytes 245792 | tf_op jit(solution)/shard_map/input_col/all_to_all | solution.py:53
  138.1 2.6 %collective-permute-start.1 = (bf16[208,1536]{1,0:T(8,128)(2,1)S(1)}, bf16[208,1536]{1,0:T(8,128)(2,1)S(1)}, u32[]{:S(2)}, u32[]{:S(2)}) collective-permute-start(bf16[208,1536]{1,0:T(8,128)(2,1)S(1)} %concatenate.16), channel_id=1, source_target_pairs={{0,128},{8,136},{16,144},{24,152},{32,160},{40,168},{48,176},{56,1... | collective-permute-start | bytes 1916936 | tf_op jit(solution)/shard_map/weight_out/ppermute | solution.py:294
  141.0 17.7 %all_to_all.49 = bf16[64,1,120]{2,1,0:T(2,128)(2,1)S(1)} all-to-all(bf16[64,1,120]{2,1,0:T(2,128)(2,1)S(1)} %all_to_all.36), channel_id=1, replica_groups={{0,10,20,30,32,42,52,62,64,74,84,94,96,106,116,126,128,138,148,158,160,..., dimensions={0} | all-to-all | bytes 30720 | tf_op jit(solution)/shard_map/input_row/all_to_all | solution.py:53
  159.1 0.7 broadcast_in_dim.33
  159.8 5.3 %all-to-all-start.7 = ((bf16[8,60,128]{2,1,0:T(8,128)(2,1)}), bf16[8,60,128]{2,1,0:T(8,128)(2,1)S(1)}, u32[]{:S(2)}, u32[]{:S(2)}) async-start(bf16[8,60,128]{2,1,0:T(8,128)(2,1)} %broadcast_in_dim.33), calls=%async_computation.7 | async-start | bytes 262144 | tf_op jit(solution)/shard_map/input_back/all_to_all | solution.py:53
  165.1 0.5 convolution_convert_fusion.w_ref
  165.6 1.1 join_halves.1
  166.7 4.2 %all-to-all-done.7.x_ref = bf16[8,60,128]{2,1,0:T(8,128)(2,1)S(1)} async-done(((bf16[8,60,128]{2,1,0:T(8,128)(2,1)}), bf16[8,60,128]{2,1,0:T(8,128)(2,1)S(1)}, u32[]{:S(2)}, u32[]{:S(2)}) %all-to-all-start.7) | async-done | bytes 122912 | tf_op jit(solution)/shard_map/input_back/all_to_all | solution.py:53
  170.9 1.1 interleave.1
  (49 shorter events, 3.2 us)
Async XLA Ops:
  0.6 26.6 %copy-start = (f32[3072]{0:T(1024)S(1)}, f32[3072]{0:T(1024)}, u32[]{:S(2)}) copy-start(f32[3072]{0:T(1024)} %param.6) | copy-start | bytes 36868
  0.6 1.2 copy-start.3
  0.7 5.2 %copy-start.2 = (bf16[5,12288]{1,0:T(8,128)(2,1)S(1)}, bf16[5,12288]{1,0:T(8,128)(2,1)}, u32[]{:S(2)}) copy-start(bf16[5,12288]{1,0:T(8,128)(2,1)} %param.4) | copy-start | bytes 368644
  1.9 25.4 %collective-permute-start = (bf16[197,1536]{1,0:T(8,128)(2,1)S(1)}, bf16[197,1536]{1,0:T(8,128)(2,1)S(1)}, u32[]{:S(2)}, u32[]{:S(2)}) collective-permute-start(bf16[197,1536]{1,0:T(8,128)(2,1)S(1)} %pad_maximum_fusion), channel_id=1, source_target_pairs={{0,128},{8,136},{16,144},{24,152},{32,160},{40,168},{48,176},{56,1... | collective-permute-start | bytes 1815560 | tf_op jit(solution)/shard_map/weight_in/ppermute | solution.py:237
  6.5 21.1 %copy-start.1 = (bf16[192,3072]{1,0:T(8,128)(2,1)S(1)}, bf16[192,3072]{1,0:T(8,128)(2,1)}, u32[]{:S(2)}) copy-start(bf16[192,3072]{1,0:T(8,128)(2,1)} %w_ref.1) | copy-start | bytes 3538948
  7.5 41.3 %all-to-all-start = ((bf16[64,16,120]{2,1,0:T(8,128)(2,1)}), bf16[64,16,120]{2,1,0:T(8,128)(2,1)S(1)}, u32[]{:S(2)}, u32[]{:S(2)}) async-start(bf16[64,16,120]{2,1,0:T(8,128)(2,1)} %pad_maximum_fusion.1), calls=%async_computation | async-start | bytes 524288 | tf_op jit(solution)/shard_map/tokens/all_to_all | solution.py:53
  117.0 21.1 %all-to-all-start.5 = ((bf16[16,24,320]{2,1,0:T(8,128)(2,1)}), bf16[16,24,320]{2,1,0:T(8,128)(2,1)S(1)}, u32[]{:S(2)}, u32[]{:S(2)}) async-start(bf16[16,24,320]{2,1,0:T(8,128)(2,1)} %bitcast.8), calls=%async_computation.5 | async-start | bytes 589824 | tf_op jit(solution)/shard_map/input_col/all_to_all | solution.py:53
  138.1 27.5 %collective-permute-start.1 = (bf16[208,1536]{1,0:T(8,128)(2,1)S(1)}, bf16[208,1536]{1,0:T(8,128)(2,1)S(1)}, u32[]{:S(2)}, u32[]{:S(2)}) collective-permute-start(bf16[208,1536]{1,0:T(8,128)(2,1)S(1)} %concatenate.16), channel_id=1, source_target_pairs={{0,128},{8,136},{16,144},{24,152},{32,160},{40,168},{48,176},{56,1... | collective-permute-start | bytes 1916936 | tf_op jit(solution)/shard_map/weight_out/ppermute | solution.py:294
  159.8 11.1 %all-to-all-start.7 = ((bf16[8,60,128]{2,1,0:T(8,128)(2,1)}), bf16[8,60,128]{2,1,0:T(8,128)(2,1)S(1)}, u32[]{:S(2)}, u32[]{:S(2)}) async-start(bf16[8,60,128]{2,1,0:T(8,128)(2,1)} %broadcast_in_dim.33), calls=%async_computation.7 | async-start | bytes 262144 | tf_op jit(solution)/shard_map/input_back/all_to_all | solution.py:53

commit v5 on v4

--- a/solution.py
+++ b/solution.py
@@ -36,6 +36,7 @@
     [row_of(p, i, y * N_Z + z) for p in range(N_PAIR) for y in range(N_YZ // N_Z)] for i in range(N_HALF) for z in range(N_Z)
 ]
 Z_GROUPS = [[q * N_Z + z for z in range(N_Z)] for q in range(N_ROW // N_Z)]
+CORES = [(c, c ^ 1) for c in range(N_COL)]
 PARTNER = [(r, r ^ N_YZ) for r in range(N_ROW)]
 
 
@@ -64,8 +65,8 @@
 
 def weight_kernel(half_ref, w_ref, got_ref, o_ref):
     panel, width = o_ref.shape[1:]
-    o_ref[0] = w_ref[:, pl.ds(pl.multiple_of(half_ref[0] * width, LANES), width)]
-    o_ref[1] = got_ref[:panel, :]
+    o_ref[half_ref[1]] = w_ref[:, pl.ds(pl.multiple_of(half_ref[0] * width, LANES), width)]
+    o_ref[1 - half_ref[1]] = got_ref[:panel, :]
 
 
 def both_panels(half, weight, got):
@@ -135,7 +136,7 @@
     s_ref[...] = g_ref[...].reshape(s_ref.shape).astype(jnp.float32)
     for j in range(lines):
         rows_ref[:, j * LANES : (j + 1) * LANES] = s_ref[pl.ds(j, rows, stride=lines), :].astype(rows_ref.dtype)
-    for k, place in enumerate((half_ref[0], 1 - half_ref[0])):
+    for k, place in enumerate((half_ref[2], 1 - half_ref[2])):
         part_ref[place] = lax.dot_general(
             w_ref[k], rows_ref[...], (((1,), (1,)), ((), ())), preferred_element_type=jnp.float32
         ).astype(part_ref.dtype)
@@ -224,7 +225,9 @@
     f32, bf16 = jnp.float32, jnp.bfloat16
     half = (lax.axis_index("row") // N_YZ) % N_HALF
     first = half == 0
-    half_ref = half.reshape(1).astype(jnp.int32)
+    core = lax.axis_index("col") % 2
+    crossed = half ^ core
+    half_ref = jnp.stack([half, crossed, core]).astype(jnp.int32)
 
     def columns(value, which):
         return lax.dynamic_slice_in_dim(value, which * width, width, value.ndim - 1)
@@ -237,22 +240,20 @@
         got = lax.ppermute(give, "row", PARTNER)
         weights = both_panels(half_ref, weight, got)
     with jax.named_scope("tokens"):
-        t = tokens.reshape(rows, N_ROW, panel).transpose(1, 0, 2).reshape(N_ROW, 8, -1)
-        flipped = t.reshape(N_PAIR, N_HALF, N_YZ, 8, -1)[:, ::-1].reshape(t.shape)
-        t = swap(jnp.concatenate([t, flipped], 1), BOTH, ROW_GROUPS)
-
-        def token_rows(value):
-            value = value.reshape(N_PAIR, N_HALF, N_YZ, rows, panel).transpose(0, 2, 1, 3, 4)
-            return value.reshape(all_rows, panel)
-
-        own, other = token_rows(t[:, :8]), token_rows(t[:, 8:])
+        t = lax.dynamic_index_in_dim(tokens.reshape(rows, N_PAIR, N_HALF, N_YZ * panel), core, 2, False)
+        t = t.reshape(rows, N_PAIR * N_YZ, panel).transpose(1, 0, 2).reshape(N_PAIR, 1, N_YZ, 8, -1)
+        t = jnp.broadcast_to(t, (N_PAIR, N_HALF) + t.shape[2:]).reshape(N_ROW, 8, -1)
+        t = swap(t, BOTH, ROW_GROUPS)
+        t = t.reshape(N_PAIR, N_HALF, N_YZ, rows, panel).transpose(0, 2, 1, 3, 4)
+        fetched = t.reshape(all_rows, panel)
+        swapped = lax.ppermute(fetched, "col", CORES)
     with jax.named_scope("pre_dot"):
         pair_rows = N_HALF * rows
         bias_half = columns(bias, half).reshape(1, -1, LANES)
         bias_rows = jnp.broadcast_to(bias_half, (pair_rows,) + bias_half.shape[1:]).reshape(-1, LANES)
         upstream = in_order(columns(grad_out, half), got[panel:], 0).reshape(-1, LANES)
-        own, other, bias_rows, upstream = lax.optimization_barrier((own, other, bias_rows, upstream))
-        partial = pre_dot(own, other, weights)
+        fetched, swapped, bias_rows, upstream = lax.optimization_barrier((fetched, swapped, bias_rows, upstream))
+        partial = pre_dot(fetched, swapped, weights)
     with jax.named_scope("pre_xy"):
         partial = swap(partial, "row", PY_GROUPS)
         partial = sum_parts(partial)
@@ -276,8 +277,10 @@
         g, part = post_dot(half_ref, g, weights)
     with jax.named_scope("weight_dot"):
         over_rows = (((0,), (0,)), ((), ()))
-        weight_own = lax.dot_general(own, g, over_rows, preferred_element_type=f32).astype(bf16)
-        weight_other = lax.dot_general(other, g, over_rows, preferred_element_type=f32).astype(bf16)
+        weight_a = lax.dot_general(fetched, g, over_rows, preferred_element_type=f32).astype(bf16)
+        weight_b = lax.dot_general(swapped, g, over_rows, preferred_element_type=f32).astype(bf16)
+        weight_own = jnp.where(crossed == 0, weight_a, weight_b)
+        weight_other = jnp.where(crossed == 0, weight_b, weight_a)
     with jax.named_scope("bias_sum"):
         bias_half = jnp.sum(g.astype(f32), axis=0)
         high = lax.reduce_precision(bias_half, 8, 7)

time: 173 us -> 175 us (1.012)
  blocking collectives: 82 us -> 69 us
  starting transfers between devices: 42.6 us -> 50.5 us
  waiting for transfers between devices: 34.3 us -> 39 us
  local copies, waits for them, and re-layouts: 5 us -> 6.78 us
    all_to_all x5 -> x4, blocking collectives: 82 us -> 69 us  [swap(): return lax.all_to_all(block, axis, 0, 0, axis_index_groups=groups)]
    all_to_all x3 -> x4, waiting for transfers between devices: 34.3 us -> 38.8 us  [swap(): return lax.all_to_all(block, axis, 0, 0, axis_index_groups=groups)]
    ppermute x0 -> x1, starting transfers between devices: none -> 4.28 us  [per_device(): swapped = lax.ppermute(fetched, 'col', CORES)]
    all_to_all x3 -> x4, starting transfers between devices: 36 us -> 39.7 us  [swap(): return lax.all_to_all(block, axis, 0, 0, axis_index_groups=groups)]
  transfers between devices with their start and end apart: 5 -> 7, of which waited for: 3 -> 5; matrix products, arithmetic and copies ran while one was open for 3% -> 3% of each run, Pallas kernels for 1% -> 1%
where the time goes in v5:
time: 175 us; the launch traced here: 174 us
  blocking collectives  69 us (39%)
  starting transfers between devices  50.5 us (29%)
  waiting for transfers between devices  39 us (22%)
  local copies, waits for them, and re-layouts  6.78 us (4%)
  Pallas kernels  5.78 us (3%)
    all_to_all x4, blocking collectives, swap(): return lax.all_to_all(block, axis, 0, 0, axis_index_groups=groups)  69 us
    all_to_all x4, starting transfers between devices, swap(): return lax.all_to_all(block, axis, 0, 0, axis_index_groups=groups)  39.7 us
    all_to_all x4, waiting for transfers between devices, swap(): return lax.all_to_all(block, axis, 0, 0, axis_index_groups=groups)  38.8 us
    ppermute x1, starting transfers between devices, per_device(): swapped = lax.ppermute(fetched, 'col', CORES)  4.28 us
    ppermute x1, starting transfers between devices, per_device(): got = lax.ppermute(give, 'row', PARTNER)  3.95 us
  transfers between devices with their start and end apart: 7, of which 5 were waited for; matrix products, arithmetic and copies ran while one was open for 3% of the time, Pallas kernels for 1%

profile of v5, /device:TPU:1, one launch (start us, length us, event | category | flops | bytes accessed | tf_op | source)
XLA Modules:
  0.0 174.3 jit_solution(6782682071683807451)
XLA Ops:
  0.7 1.1 constant_dynamic-slice_fusion.1
  1.9 3.9 %collective-permute-start.1 = (bf16[197,1536]{1,0:T(8,128)(2,1)S(1)}, bf16[197,1536]{1,0:T(8,128)(2,1)S(1)}, u32[]{:S(2)}, u32[]{:S(2)}) collective-permute-start(bf16[197,1536]{1,0:T(8,128)(2,1)S(1)} %pad_maximum_fusion), channel_id=1, source_target_pairs={{0,128},{8,136},{16,144},{24,152},{32,160},{40,168},{48,176},{56,1... | collective-permute-start | bytes 1815560 | tf_op jit(solution)/shard_map/weight_in/ppermute | solution.py:240
  6.7 0.7 broadcast_in_dim.35
  7.4 19.7 %all-to-all-start = ((bf16[64,8,120]{2,1,0:T(8,128)(2,1)}), bf16[64,8,120]{2,1,0:T(8,128)(2,1)S(1)}, u32[]{:S(2)}, u32[]{:S(2)}) async-start(bf16[64,8,120]{2,1,0:T(8,128)(2,1)} %bitcast.4), calls=%async_computation | async-start | bytes 262144 | tf_op jit(solution)/shard_map/tokens/all_to_all | solution.py:54
  27.3 15.5 %all-to-all-done = bf16[64,8,120]{2,1,0:T(8,128)(2,1)S(1)} async-done(((bf16[64,8,120]{2,1,0:T(8,128)(2,1)}), bf16[64,8,120]{2,1,0:T(8,128)(2,1)S(1)}, u32[]{:S(2)}, u32[]{:S(2)}) %all-to-all-start) | async-done | bytes 122912 | tf_op jit(solution)/shard_map/tokens/all_to_all | solution.py:54
  43.2 4.3 %collective-permute-start = (bf16[320,192]{1,0:T(8,128)(2,1)S(1)}, bf16[320,192]{1,0:T(8,128)(2,1)S(1)}, u32[]{:S(2)}, u32[]{:S(2)}) collective-permute-start(bf16[320,192]{1,0:T(8,128)(2,1)S(1)} %reshape.91.own_ref), channel_id=1, source_target_pairs={{0,1},{1,0},{2,3},{3,2},{4,5},{5,4},{6,7},{7,6},{8,9},{9,8},{10,11... | collective-permute-start | bytes 368648 | tf_op jit(solution)/shard_map/tokens/ppermute | solution.py:249
  48.5 0.7 pre_dot.1
  49.2 18.2 %all_to_all.45.x_ref = bf16[8,480,128]{2,1,0:T(8,128)(2,1)S(1)} all-to-all(bf16[8,480,128]{2,1,0:T(8,128)(2,1)S(1)} %pre_dot.1), channel_id=1, replica_groups={{0,32,64,96,256,288,320,352},{8,40,72,104,264,296,328,360},{16,48,80,11..., dimensions={0} | all-to-all | bytes 1966080 | tf_op jit(solution)/shard_map/pre_xy/all_to_all | solution.py:54
  67.5 16.3 %all_to_all.46 = bf16[4,120,128]{2,1,0:T(8,128)(2,1)S(1)} all-to-all(bf16[4,120,128]{2,1,0:T(8,128)(2,1)S(1)} %bitcast.28), channel_id=1, replica_groups={{0,8,16,24},{32,40,48,56},{64,72,80,88},{96,104,112,120},{128,136,144,1..., dimensions={0} | all-to-all | bytes 245760 | tf_op jit(solution)/shard_map/pre_z/all_to_all | solution.py:54
  84.6 15.2 %all_to_all.47 = bf16[4,120,128]{2,1,0:T(8,128)(2,1)S(1)} all-to-all(bf16[4,120,128]{2,1,0:T(8,128)(2,1)S(1)} %broadcast_in_dim.38), channel_id=1, replica_groups={{0,8,16,24},{32,40,48,56},{64,72,80,88},{96,104,112,120},{128,136,144,1..., dimensions={0} | all-to-all | bytes 245760 | tf_op jit(solution)/shard_map/grad_z/all_to_all | solution.py:54
  99.8 1.1 broadcast_in_dim.40
  100.9 3.9 %all-to-all-start.4 = ((bf16[8,480,128]{2,1,0:T(8,128)(2,1)}), bf16[8,480,128]{2,1,0:T(8,128)(2,1)S(1)}, u32[]{:S(2)}, u32[]{:S(2)}) async-start(bf16[8,480,128]{2,1,0:T(8,128)(2,1)} %broadcast_in_dim.40), calls=%async_computation.4 | async-start | bytes 1966080 | tf_op jit(solution)/shard_map/grad_xy/all_to_all | solution.py:54
  104.7 10.6 %all-to-all-done.4.g_ref = bf16[8,480,128]{2,1,0:T(8,128)(2,1)S(1)} async-done(((bf16[8,480,128]{2,1,0:T(8,128)(2,1)}), bf16[8,480,128]{2,1,0:T(8,128)(2,1)S(1)}, u32[]{:S(2)}, u32[]{:S(2)}) %all-to-all-start.4) | async-done | bytes 983072 | tf_op jit(solution)/shard_map/grad_xy/all_to_all | solution.py:54
  115.3 1.6 post_dot.1
  117.0 0.7 copy-done.2
  117.9 10.7 %all-to-all-start.5 = ((bf16[16,24,320]{2,1,0:T(8,128)(2,1)}), bf16[16,24,320]{2,1,0:T(8,128)(2,1)S(1)}, u32[]{:S(2)}, u32[]{:S(2)}) async-start(bf16[16,24,320]{2,1,0:T(8,128)(2,1)} %bitcast.29), calls=%async_computation.5 | async-start | bytes 589824 | tf_op jit(solution)/shard_map/input_col/all_to_all | solution.py:54
  129.9 8.6 %all-to-all-done.5 = bf16[16,24,320]{2,1,0:T(8,128)(2,1)S(1)} async-done(((bf16[16,24,320]{2,1,0:T(8,128)(2,1)}), bf16[16,24,320]{2,1,0:T(8,128)(2,1)S(1)}, u32[]{:S(2)}, u32[]{:S(2)}) %all-to-all-start.5) | async-done | bytes 245792 | tf_op jit(solution)/shard_map/input_col/all_to_all | solution.py:54
  138.6 2.6 %collective-permute-start.2 = (bf16[208,1536]{1,0:T(8,128)(2,1)S(1)}, bf16[208,1536]{1,0:T(8,128)(2,1)S(1)}, u32[]{:S(2)}, u32[]{:S(2)}) collective-permute-start(bf16[208,1536]{1,0:T(8,128)(2,1)S(1)} %concatenate.12), channel_id=1, source_target_pairs={{0,128},{8,136},{16,144},{24,152},{32,160},{40,168},{48,176},{56,1... | collective-permute-start | bytes 1916936 | tf_op jit(solution)/shard_map/weight_out/ppermute | solution.py:297
  141.6 19.3 %all_to_all.48 = bf16[64,1,120]{2,1,0:T(2,128)(2,1)S(1)} all-to-all(bf16[64,1,120]{2,1,0:T(2,128)(2,1)S(1)} %all_to_all.36), channel_id=1, replica_groups={{0,10,20,30,32,42,52,62,64,74,84,94,96,106,116,126,128,138,148,158,160,..., dimensions={0} | all-to-all | bytes 30720 | tf_op jit(solution)/shard_map/input_row/all_to_all | solution.py:54
  161.3 0.7 broadcast_in_dim.42
  162.0 5.4 %all-to-all-start.7 = ((bf16[8,60,128]{2,1,0:T(8,128)(2,1)}), bf16[8,60,128]{2,1,0:T(8,128)(2,1)S(1)}, u32[]{:S(2)}, u32[]{:S(2)}) async-start(bf16[8,60,128]{2,1,0:T(8,128)(2,1)} %broadcast_in_dim.42), calls=%async_computation.7 | async-start | bytes 262144 | tf_op jit(solution)/shard_map/input_back/all_to_all | solution.py:54
  167.4 1.6 join_halves.1
  169.1 4.1 %all-to-all-done.7.x_ref = bf16[8,60,128]{2,1,0:T(8,128)(2,1)S(1)} async-done(((bf16[8,60,128]{2,1,0:T(8,128)(2,1)}), bf16[8,60,128]{2,1,0:T(8,128)(2,1)S(1)}, u32[]{:S(2)}, u32[]{:S(2)}) %all-to-all-start.7) | async-done | bytes 122912 | tf_op jit(solution)/shard_map/input_back/all_to_all | solution.py:54
  173.2 1.1 interleave.1
  (54 shorter events, 5.6 us)
Async XLA Ops:
  0.6 26.5 %copy-start = (f32[3072]{0:T(1024)S(1)}, f32[3072]{0:T(1024)}, u32[]{:S(2)}) copy-start(f32[3072]{0:T(1024)} %param.6) | copy-start | bytes 36868
  0.6 1.2 copy-start.5
  0.7 5.2 %copy-start.3 = (bf16[5,12288]{1,0:T(8,128)(2,1)S(1)}, bf16[5,12288]{1,0:T(8,128)(2,1)}, u32[]{:S(2)}) copy-start(bf16[5,12288]{1,0:T(8,128)(2,1)} %param.4) | copy-start | bytes 368644
  1.9 45.6 %collective-permute-start.1 = (bf16[197,1536]{1,0:T(8,128)(2,1)S(1)}, bf16[197,1536]{1,0:T(8,128)(2,1)S(1)}, u32[]{:S(2)}, u32[]{:S(2)}) collective-permute-start(bf16[197,1536]{1,0:T(8,128)(2,1)S(1)} %pad_maximum_fusion), channel_id=1, source_target_pairs={{0,128},{8,136},{16,144},{24,152},{32,160},{40,168},{48,176},{56,1... | collective-permute-start | bytes 1815560 | tf_op jit(solution)/shard_map/weight_in/ppermute | solution.py:240
  6.7 41.0 %copy-start.1 = (bf16[192,3072]{1,0:T(8,128)(2,1)S(1)}, bf16[192,3072]{1,0:T(8,128)(2,1)}, u32[]{:S(2)}) copy-start(bf16[192,3072]{1,0:T(8,128)(2,1)} %w_ref.1) | copy-start | bytes 3538948
  7.4 35.4 %all-to-all-start = ((bf16[64,8,120]{2,1,0:T(8,128)(2,1)}), bf16[64,8,120]{2,1,0:T(8,128)(2,1)S(1)}, u32[]{:S(2)}, u32[]{:S(2)}) async-start(bf16[64,8,120]{2,1,0:T(8,128)(2,1)} %bitcast.4), calls=%async_computation | async-start | bytes 262144 | tf_op jit(solution)/shard_map/tokens/all_to_all | solution.py:54
  43.2 5.3 %collective-permute-start = (bf16[320,192]{1,0:T(8,128)(2,1)S(1)}, bf16[320,192]{1,0:T(8,128)(2,1)S(1)}, u32[]{:S(2)}, u32[]{:S(2)}) collective-permute-start(bf16[320,192]{1,0:T(8,128)(2,1)S(1)} %reshape.91.own_ref), channel_id=1, source_target_pairs={{0,1},{1,0},{2,3},{3,2},{4,5},{5,4},{6,7},{7,6},{8,9},{9,8},{10,11... | collective-permute-start | bytes 368648 | tf_op jit(solution)/shard_map/tokens/ppermute | solution.py:249
  100.9 14.5 %all-to-all-start.4 = ((bf16[8,480,128]{2,1,0:T(8,128)(2,1)}), bf16[8,480,128]{2,1,0:T(8,128)(2,1)S(1)}, u32[]{:S(2)}, u32[]{:S(2)}) async-start(bf16[8,480,128]{2,1,0:T(8,128)(2,1)} %broadcast_in_dim.40), calls=%async_computation.4 | async-start | bytes 1966080 | tf_op jit(solution)/shard_map/grad_xy/all_to_all | solution.py:54
  104.7 13.1 %copy-start.4 = (bf16[120,128]{1,0:T(8,128)(2,1)S(1)}, bf16[120,128]{1,0:T(8,128)(2,1)}, u32[]{:S(2)}) copy-start(bf16[120,128]{1,0:T(8,128)(2,1)} %get-tuple-element.32) | copy-start | bytes 92164
  116.9 0.7 copy-start.2
  117.9 20.7 %all-to-all-start.5 = ((bf16[16,24,320]{2,1,0:T(8,128)(2,1)}), bf16[16,24,320]{2,1,0:T(8,128)(2,1)S(1)}, u32[]{:S(2)}, u32[]{:S(2)}) async-start(bf16[16,24,320]{2,1,0:T(8,128)(2,1)} %bitcast.29), calls=%async_computation.5 | async-start | bytes 589824 | tf_op jit(solution)/shard_map/input_col/all_to_all | solution.py:54
  138.6 28.8 %collective-permute-start.2 = (bf16[208,1536]{1,0:T(8,128)(2,1)S(1)}, bf16[208,1536]{1,0:T(8,128)(2,1)S(1)}, u32[]{:S(2)}, u32[]{:S(2)}) collective-permute-start(bf16[208,1536]{1,0:T(8,128)(2,1)S(1)} %concatenate.12), channel_id=1, source_target_pairs={{0,128},{8,136},{16,144},{24,152},{32,160},{40,168},{48,176},{56,1... | collective-permute-start | bytes 1916936 | tf_op jit(solution)/shard_map/weight_out/ppermute | solution.py:297
  162.0 11.3 %all-to-all-start.7 = ((bf16[8,60,128]{2,1,0:T(8,128)(2,1)}), bf16[8,60,128]{2,1,0:T(8,128)(2,1)S(1)}, u32[]{:S(2)}, u32[]{:S(2)}) async-start(bf16[8,60,128]{2,1,0:T(8,128)(2,1)} %broadcast_in_dim.42), calls=%async_computation.7 | async-start | bytes 262144 | tf_op jit(solution)/shard_map/input_back/all_to_all | solution.py:54

commit v6 on v4

--- a/solution.py
+++ b/solution.py
@@ -284,14 +284,14 @@
         middle = lax.reduce_precision(bias_half - high, 8, 7)
         low = bias_half - high - middle
         pieces = jnp.stack([high, middle, low] + [jnp.zeros_like(low)] * (TAIL - rows - 3)).astype(bf16)
+    with jax.named_scope("weight_out"):
+        give = jnp.concatenate([weight_other, lax.dynamic_index_in_dim(activation, 1 - half, 0, False), pieces], 0)
+        part, give = lax.optimization_barrier((part, give))
+        back = lax.ppermute(give, "row", PARTNER)
     with jax.named_scope("input_col"):
         slim = panel // N_COL
         part = swap(part.reshape(N_HALF * N_COL, slim, all_rows), BOTH, PAIR_COL_GROUPS)
         part = jnp.sum(part.astype(f32), axis=0).astype(bf16)
-    with jax.named_scope("weight_out"):
-        give = jnp.concatenate([weight_other, lax.dynamic_index_in_dim(activation, 1 - half, 0, False), pieces], 0)
-        part, give = lax.optimization_barrier((part, give))
-        back = lax.ppermute(give, "row", PARTNER)
     with jax.named_scope("input_row"):
         part = part.reshape(slim, N_PAIR, N_YZ, N_HALF, rows).transpose(1, 3, 2, 4, 0).reshape(N_ROW, rows * slim)
         part = swap(part, BOTH, ROW_GROUPS)

time: 173 us -> 173 us (level)
  blocking collectives: 82 us -> 67.4 us
  waiting for transfers between devices: 34.3 us -> 42.1 us
  starting transfers between devices: 42.6 us -> 47.8 us
    all_to_all x5 -> x4, blocking collectives: 82 us -> 67.4 us  [swap(): return lax.all_to_all(block, axis, 0, 0, axis_index_groups=groups)]
    all_to_all x3 -> x4, waiting for transfers between devices: 34.3 us -> 42.1 us  [swap(): return lax.all_to_all(block, axis, 0, 0, axis_index_groups=groups)]
    all_to_all x3 -> x4, starting transfers between devices: 36 us -> 40.5 us  [swap(): return lax.all_to_all(block, axis, 0, 0, axis_index_groups=groups)]
  transfers between devices with their start and end apart: 5 -> 6, of which waited for: 3 -> 4; matrix products, arithmetic and copies ran while one was open for 3% -> 2% of each run, Pallas kernels for 1% -> 1%
where the time goes in v6:
time: 173 us
  blocking collectives  67.4 us (39%)
  starting transfers between devices  47.8 us (28%)
  waiting for transfers between devices  42.1 us (24%)
  local copies, waits for them, and re-layouts  6.62 us (4%)
  Pallas kernels  4.87 us (3%)
  other arithmetic  1.76 us (1%)
    all_to_all x4, blocking collectives, swap(): return lax.all_to_all(block, axis, 0, 0, axis_index_groups=groups)  67.4 us
    all_to_all x4, waiting for transfers between devices, swap(): return lax.all_to_all(block, axis, 0, 0, axis_index_groups=groups)  42.1 us
    all_to_all x4, starting transfers between devices, swap(): return lax.all_to_all(block, axis, 0, 0, axis_index_groups=groups)  40.5 us
    ppermute x1, starting transfers between devices, per_device(): got = lax.ppermute(give, 'row', PARTNER)  3.95 us
  transfers between devices with their start and end apart: 6, of which 4 were waited for; matrix products, arithmetic and copies ran while one was open for 2% of the time, Pallas kernels for 1%

profile of v6, /device:TPU:1, one launch (start us, length us, event | category | flops | bytes accessed | tf_op | source)
XLA Modules:
  0.0 172.5 jit_solution(13611339495105456976)
XLA Ops:
  0.7 1.1 constant_dynamic-slice_fusion.1
  1.9 3.9 %collective-permute-start = (bf16[197,1536]{1,0:T(8,128)(2,1)S(1)}, bf16[197,1536]{1,0:T(8,128)(2,1)S(1)}, u32[]{:S(2)}, u32[]{:S(2)}) collective-permute-start(bf16[197,1536]{1,0:T(8,128)(2,1)S(1)} %pad_maximum_fusion), channel_id=1, source_target_pairs={{0,128},{8,136},{16,144},{24,152},{32,160},{40,168},{48,176},{56,1... | collective-permute-start | bytes 1815560 | tf_op jit(solution)/shard_map/weight_in/ppermute | solution.py:237
  6.8 0.8 pad_maximum_fusion.1
  7.5 19.7 %all-to-all-start = ((bf16[64,16,120]{2,1,0:T(8,128)(2,1)}), bf16[64,16,120]{2,1,0:T(8,128)(2,1)S(1)}, u32[]{:S(2)}, u32[]{:S(2)}) async-start(bf16[64,16,120]{2,1,0:T(8,128)(2,1)} %pad_maximum_fusion.1), calls=%async_computation | async-start | bytes 524288 | tf_op jit(solution)/shard_map/tokens/all_to_all | solution.py:53
  27.4 0.7 reshape.106
  28.2 20.6 %all-to-all-done = bf16[64,16,120]{2,1,0:T(8,128)(2,1)S(1)} async-done(((bf16[64,16,120]{2,1,0:T(8,128)(2,1)}), bf16[64,16,120]{2,1,0:T(8,128)(2,1)S(1)}, u32[]{:S(2)}, u32[]{:S(2)}) %all-to-all-start) | async-done | bytes 245792 | tf_op jit(solution)/shard_map/tokens/all_to_all | solution.py:53
  49.8 0.7 pre_dot.1
  50.5 16.3 %all_to_all.45.x_ref = bf16[8,480,128]{2,1,0:T(8,128)(2,1)S(1)} all-to-all(bf16[8,480,128]{2,1,0:T(8,128)(2,1)S(1)} %pre_dot.1), channel_id=1, replica_groups={{0,32,64,96,256,288,320,352},{8,40,72,104,264,296,328,360},{16,48,80,11..., dimensions={0} | all-to-all | bytes 1966080 | tf_op jit(solution)/shard_map/pre_xy/all_to_all | solution.py:53
  66.9 17.9 %all_to_all.46 = bf16[4,120,128]{2,1,0:T(8,128)(2,1)S(1)} all-to-all(bf16[4,120,128]{2,1,0:T(8,128)(2,1)S(1)} %bitcast.27), channel_id=1, replica_groups={{0,8,16,24},{32,40,48,56},{64,72,80,88},{96,104,112,120},{128,136,144,1..., dimensions={0} | all-to-all | bytes 245760 | tf_op jit(solution)/shard_map/pre_z/all_to_all | solution.py:53
  84.9 0.7 fusion.6
  85.5 14.8 %all_to_all.47 = bf16[4,120,128]{2,1,0:T(8,128)(2,1)S(1)} all-to-all(bf16[4,120,128]{2,1,0:T(8,128)(2,1)S(1)} %broadcast_in_dim.29), channel_id=1, replica_groups={{0,8,16,24},{32,40,48,56},{64,72,80,88},{96,104,112,120},{128,136,144,1..., dimensions={0} | all-to-all | bytes 245760 | tf_op jit(solution)/shard_map/grad_z/all_to_all | solution.py:53
  100.3 1.1 broadcast_in_dim.31
  101.4 4.0 %all-to-all-start.4 = ((bf16[8,480,128]{2,1,0:T(8,128)(2,1)}), bf16[8,480,128]{2,1,0:T(8,128)(2,1)S(1)}, u32[]{:S(2)}, u32[]{:S(2)}) async-start(bf16[8,480,128]{2,1,0:T(8,128)(2,1)} %broadcast_in_dim.31), calls=%async_computation.4 | async-start | bytes 1966080 | tf_op jit(solution)/shard_map/grad_xy/all_to_all | solution.py:53
  105.4 10.5 %all-to-all-done.4.g_ref = bf16[8,480,128]{2,1,0:T(8,128)(2,1)S(1)} async-done(((bf16[8,480,128]{2,1,0:T(8,128)(2,1)}), bf16[8,480,128]{2,1,0:T(8,128)(2,1)S(1)}, u32[]{:S(2)}, u32[]{:S(2)}) %all-to-all-start.4) | async-done | bytes 983072 | tf_op jit(solution)/shard_map/grad_xy/all_to_all | solution.py:53
  115.9 1.8 %post_dot.1 = (bf16[320,1536]{1,0:T(8,128)(2,1)S(1)}, bf16[2,192,320]{2,1,0:T(8,128)(2,1)}) custom-call(s32[1]{0:T(128)} %bitcast.half_ref, bf16[8,480,128]{2,1,0:T(8,128)(2,1)S(1)} %all-to-all-done.4.g_ref, bf16[2,192,1536]{2,1,0:T(8,128)(2,1)S(1)} %both_panels.1.w_ref), custom_call_target="tpu_custom_call" | custom-call | flops 377487360 | bytes 6291456 | tf_op jit(solution)/shard_map/input_dot/post_dot/pallas_call | solution.py:147
  118.9 11.3 %all-to-all-start.5 = ((bf16[16,24,320]{2,1,0:T(8,128)(2,1)}), bf16[16,24,320]{2,1,0:T(8,128)(2,1)S(1)}, u32[]{:S(2)}, u32[]{:S(2)}) async-start(bf16[16,24,320]{2,1,0:T(8,128)(2,1)} %bitcast.9), calls=%async_computation.5 | async-start | bytes 589824 | tf_op jit(solution)/shard_map/input_col/all_to_all | solution.py:53
  130.2 3.3 %collective-permute-start.1 = (bf16[208,1536]{1,0:T(8,128)(2,1)S(1)}, bf16[208,1536]{1,0:T(8,128)(2,1)S(1)}, u32[]{:S(2)}, u32[]{:S(2)}) collective-permute-start(bf16[208,1536]{1,0:T(8,128)(2,1)S(1)} %concatenate.16), channel_id=1, source_target_pairs={{0,128},{8,136},{16,144},{24,152},{32,160},{40,168},{48,176},{56,1... | collective-permute-start | bytes 1916936 | tf_op jit(solution)/shard_map/weight_out/ppermute | solution.py:290
  133.5 6.8 %all-to-all-done.5 = bf16[16,24,320]{2,1,0:T(8,128)(2,1)S(1)} async-done(((bf16[16,24,320]{2,1,0:T(8,128)(2,1)}), bf16[16,24,320]{2,1,0:T(8,128)(2,1)S(1)}, u32[]{:S(2)}, u32[]{:S(2)}) %all-to-all-start.5) | async-done | bytes 245792 | tf_op jit(solution)/shard_map/input_col/all_to_all | solution.py:53
  140.6 18.4 %all_to_all.48 = bf16[64,1,120]{2,1,0:T(2,128)(2,1)S(1)} all-to-all(bf16[64,1,120]{2,1,0:T(2,128)(2,1)S(1)} %all_to_all.36), channel_id=1, replica_groups={{0,10,20,30,32,42,52,62,64,74,84,94,96,106,116,126,128,138,148,158,160,..., dimensions={0} | all-to-all | bytes 30720 | tf_op jit(solution)/shard_map/input_row/all_to_all | solution.py:53
  159.4 0.7 broadcast_in_dim.33
  160.1 5.5 %all-to-all-start.7 = ((bf16[8,60,128]{2,1,0:T(8,128)(2,1)}), bf16[8,60,128]{2,1,0:T(8,128)(2,1)S(1)}, u32[]{:S(2)}, u32[]{:S(2)}) async-start(bf16[8,60,128]{2,1,0:T(8,128)(2,1)} %broadcast_in_dim.33), calls=%async_computation.7 | async-start | bytes 262144 | tf_op jit(solution)/shard_map/input_back/all_to_all | solution.py:53
  166.1 1.1 join_halves.1
  167.3 4.2 %all-to-all-done.7.x_ref = bf16[8,60,128]{2,1,0:T(8,128)(2,1)S(1)} async-done(((bf16[8,60,128]{2,1,0:T(8,128)(2,1)}), bf16[8,60,128]{2,1,0:T(8,128)(2,1)S(1)}, u32[]{:S(2)}, u32[]{:S(2)}) %all-to-all-start.7) | async-done | bytes 122912 | tf_op jit(solution)/shard_map/input_back/all_to_all | solution.py:53
  171.5 1.1 interleave.1
  (54 shorter events, 4.6 us)
Async XLA Ops:
  0.6 26.6 %copy-start = (f32[3072]{0:T(1024)S(1)}, f32[3072]{0:T(1024)}, u32[]{:S(2)}) copy-start(f32[3072]{0:T(1024)} %param.6) | copy-start | bytes 36868
  0.6 1.2 copy-start.5
  0.7 5.2 %copy-start.2 = (bf16[5,12288]{1,0:T(8,128)(2,1)S(1)}, bf16[5,12288]{1,0:T(8,128)(2,1)}, u32[]{:S(2)}) copy-start(bf16[5,12288]{1,0:T(8,128)(2,1)} %param.4) | copy-start | bytes 368644
  1.9 25.4 %collective-permute-start = (bf16[197,1536]{1,0:T(8,128)(2,1)S(1)}, bf16[197,1536]{1,0:T(8,128)(2,1)S(1)}, u32[]{:S(2)}, u32[]{:S(2)}) collective-permute-start(bf16[197,1536]{1,0:T(8,128)(2,1)S(1)} %pad_maximum_fusion), channel_id=1, source_target_pairs={{0,128},{8,136},{16,144},{24,152},{32,160},{40,168},{48,176},{56,1... | collective-permute-start | bytes 1815560 | tf_op jit(solution)/shard_map/weight_in/ppermute | solution.py:237
  6.5 21.7 %copy-start.1 = (bf16[192,3072]{1,0:T(8,128)(2,1)S(1)}, bf16[192,3072]{1,0:T(8,128)(2,1)}, u32[]{:S(2)}) copy-start(bf16[192,3072]{1,0:T(8,128)(2,1)} %w_ref.1) | copy-start | bytes 3538948
  7.5 41.3 %all-to-all-start = ((bf16[64,16,120]{2,1,0:T(8,128)(2,1)}), bf16[64,16,120]{2,1,0:T(8,128)(2,1)S(1)}, u32[]{:S(2)}, u32[]{:S(2)}) async-start(bf16[64,16,120]{2,1,0:T(8,128)(2,1)} %pad_maximum_fusion.1), calls=%async_computation | async-start | bytes 524288 | tf_op jit(solution)/shard_map/tokens/all_to_all | solution.py:53
  66.8 18.1 %copy-start.4 = (bf16[120,128]{1,0:T(8,128)(2,1)S(1)}, bf16[120,128]{1,0:T(8,128)(2,1)}, u32[]{:S(2)}) copy-start(bf16[120,128]{1,0:T(8,128)(2,1)} %reshape.106) | copy-start | bytes 92164
  101.4 14.5 %all-to-all-start.4 = ((bf16[8,480,128]{2,1,0:T(8,128)(2,1)}), bf16[8,480,128]{2,1,0:T(8,128)(2,1)S(1)}, u32[]{:S(2)}, u32[]{:S(2)}) async-start(bf16[8,480,128]{2,1,0:T(8,128)(2,1)} %broadcast_in_dim.31), calls=%async_computation.4 | async-start | bytes 1966080 | tf_op jit(solution)/shard_map/grad_xy/all_to_all | solution.py:53
  117.7 0.8 copy-start.3
  118.9 21.4 %all-to-all-start.5 = ((bf16[16,24,320]{2,1,0:T(8,128)(2,1)}), bf16[16,24,320]{2,1,0:T(8,128)(2,1)S(1)}, u32[]{:S(2)}, u32[]{:S(2)}) async-start(bf16[16,24,320]{2,1,0:T(8,128)(2,1)} %bitcast.9), calls=%async_computation.5 | async-start | bytes 589824 | tf_op jit(solution)/shard_map/input_col/all_to_all | solution.py:53
  130.2 35.9 %collective-permute-start.1 = (bf16[208,1536]{1,0:T(8,128)(2,1)S(1)}, bf16[208,1536]{1,0:T(8,128)(2,1)S(1)}, u32[]{:S(2)}, u32[]{:S(2)}) collective-permute-start(bf16[208,1536]{1,0:T(8,128)(2,1)S(1)} %concatenate.16), channel_id=1, source_target_pairs={{0,128},{8,136},{16,144},{24,152},{32,160},{40,168},{48,176},{56,1... | collective-permute-start | bytes 1916936 | tf_op jit(solution)/shard_map/weight_out/ppermute | solution.py:290
  160.1 11.3 %all-to-all-start.7 = ((bf16[8,60,128]{2,1,0:T(8,128)(2,1)}), bf16[8,60,128]{2,1,0:T(8,128)(2,1)S(1)}, u32[]{:S(2)}, u32[]{:S(2)}) async-start(bf16[8,60,128]{2,1,0:T(8,128)(2,1)} %broadcast_in_dim.33), calls=%async_computation.7 | async-start | bytes 262144 | tf_op jit(solution)/shard_map/input_back/all_to_all | solution.py:53
